TPU v7x, 512 devices: a whole 4x8x8 slice. The times are simulated.
512 devices in a mesh: dom: 16 (over z, core), field: 32 (over y, x).
Axes of the slice: x: 4, y: 8, z: 8, core: 2. Of those that a mesh axis runs over, the one named last changes fastest.
Arguments:
- particles: bfloat16 [2048, 32768], P('dom', 'field'), may hold values from -12 to 12
- gradients: bfloat16 [2048, 32768], P('dom', 'field'), may hold values from -0.009765625 to 0.009765625
- kernel_scale: float32 [1], replicated, may hold values from 1966.08 to 2949.12
Outputs:
- velocity: float32 [2048, 32768], P('dom', 'field')
All inputs are finite; a program needn't handle non-finite values.
Results may differ from a plain program's by a relative error of at most 0.0005.
Values may be sent and summed in bfloat16 or wider, within the bound.
No kernel may reach another device: no remote copies, remote signals or barrier semaphores. Data moves between devices by JAX's collectives and lax.ppermute only.
A program may use at most 64 MiB of HBM per device.

v0:
```python
import jax
import jax.numpy as jnp
from jax import lax
from jax.sharding import PartitionSpec as P


def cross_rows(left, right):
    return lax.dot_general(
        left, right, (((1,), (1,)), ((), ())), preferred_element_type=jnp.float32
    )


def squares_of(block):
    wide = block.astype(jnp.float32)
    return jnp.sum(wide * wide, axis=1)


def on_device(particles, gradients, kernel_scale):
    rows = particles.shape[0]
    scale = kernel_scale[0]
    all_coords, all_grads = (
        lax.all_gather(particles, "dom", axis=0, tiled=True),
        lax.all_gather(gradients, "dom", axis=0, tiled=True),
    )
    partial_value = cross_rows(particles, all_coords)
    squares = squares_of(all_coords)
    gram, norms = lax.psum((partial_value, squares), "field")
    own_norms = lax.dynamic_slice_in_dim(norms, lax.axis_index("dom") * rows, rows, 0)
    dist = jnp.maximum(own_norms[:, None] + norms[None, :] - 2.0 * gram, 0.0)
    kernel = jnp.exp(-dist / scale).astype(jnp.bfloat16)
    weight = jnp.sum(kernel.astype(jnp.float32), axis=1)
    pulled = jnp.dot(kernel, all_grads, preferred_element_type=jnp.float32)
    spread = jnp.dot(kernel, all_coords, preferred_element_type=jnp.float32)
    coords = particles.astype(jnp.float32)
    return (0.5 * scale * pulled - spread + weight[:, None] * coords) / weight[:, None]


def solution(mesh):
    placed = (P("dom", "field"), P("dom", "field"), P())
    return jax.shard_map(
        on_device, mesh=mesh, in_specs=placed, out_specs=P("dom", "field"), check_vma=False
    )
```

profile of v0, /device:TPU:1, one launch (start us, length us, event | category | flops | bytes accessed | tf_op | source)
XLA Modules:
  0.0 281.7 jit_solution(6234386341650356838)
XLA Ops:
  6.5 0.0 all-gather.3.cloned.1.call-start
  6.5 0.7 all-gather.3.cloned.1.call-update
  7.3 0.0 all-reduce.2.cloned.1.call-start
  7.3 53.8 %all-gather.3.cloned.1.call-done = bf16[2048,1024]{1,0:T(8,128)(2,1)} async-done(((bf16[128,1024]{1,0:T(8,128)(2,1)}), bf16[2048,1024]{1,0:T(8,128)(2,1)}) %all-gather.3.cloned.1.call-update) | async-done | bytes 4194320 | tf_op jit(solution)/shard_map/all_gather | solution.py:22
  61.1 4.8 %fusion.2 = f32[128,2048]{1,0:T(8,128)} fusion(bf16[128,1024]{1,0:T(8,128)(2,1)} %param.3, bf16[2048,1024]{1,0:T(8,128)(2,1)} %all-gather.3.cloned.1.call-done), kind=kOutput, calls=%fused_computation.7 | convolution fusion | flops 536870912 | bytes 5505024 | tf_op jit(solution)/shard_map/dot_general | solution.py:8
  65.9 0.0 all-reduce.2.cloned.1.call-update
  65.9 0.0 all-gather.5.cloned.1.call-start
  65.9 0.7 all-gather.5.cloned.1.call-update
  67.3 3.1 %multiply_reduce_fusion = f32[2048]{0:T(1024)S(1)} fusion(bf16[2048,1024]{1,0:T(8,128)(2,1)} %all-gather.3.cloned.1.call-done), kind=kLoop, calls=%fused_computation | loop fusion | flops 6289408 | bytes 4202496 | tf_op jit(solution)/shard_map/reduce_sum | solution.py:15
  70.3 0.0 copy-start.1
  70.4 61.8 %psum.14 = f32[2048]{0:T(1024)S(1)} all-reduce(f32[2048]{0:T(1024)S(1)} %multiply_reduce_fusion), channel_id=1, replica_groups=mesh['dom'=16,'field'=32] {'field'}, use_global_device_ids=true, to_apply=%region_1.0 | all-reduce | flops 2048 | bytes 16384 | tf_op jit(solution)/shard_map/psum | solution.py:27
  132.2 0.1 dynamic_slice.3
  132.3 87.4 %all-reduce.2.cloned.1.call-done = f32[128,2048]{1,0:T(8,128)} async-done(((f32[128,2048]{1,0:T(8,128)}), f32[128,2048]{1,0:T(8,128)}) %all-reduce.2.cloned.1.call-update) | async-done | bytes 1048592 | tf_op jit(solution)/shard_map/psum | solution.py:27
  219.7 1.7 convert_reduce_fusion
  221.4 48.7 %all-gather.5.cloned.1.call-done = bf16[2048,1024]{1,0:T(8,128)(2,1)} async-done(((bf16[128,1024]{1,0:T(8,128)(2,1)}), bf16[2048,1024]{1,0:T(8,128)(2,1)}) %all-gather.5.cloned.1.call-update) | async-done | bytes 4194320 | tf_op jit(solution)/shard_map/all_gather | solution.py:23
  270.1 0.0 copy-start
  270.1 3.1 %convolution_multiply_fusion = f32[128,1024]{1,0:T(8,128)S(1)} fusion(bf16[128,2048]{1,0:T(8,128)(2,1)S(1)} %get-tuple-element.6, bf16[2048,1024]{1,0:T(8,128)(2,1)} %all-gather.5.cloned.1.call-done, f32[]{:T(128)S(6)} %mul_shard_map.3), kind=kOutput, calls=%fused_computation.2 | convolution fusion | flops 537001984 | bytes 5242884 | tf_op jit(solution)/shard_map/dot_general | solution.py:32
  273.2 0.0 copy-done.1
  273.2 0.4 copy-done
  273.6 1.6 fusion.1
Async XLA Ops:
  6.5 54.6 %all-gather.3.cloned.1.call-start = ((), (), s32[]{:S(2)}) async-start(), calls=%async_computation | async-start | bytes 4456448 | tf_op jit(solution)/shard_map/all_gather | solution.py:22
  7.3 212.4 %all-reduce.2.cloned.1.call-start = ((), (), s32[]{:S(2)}) async-start(), calls=%async_computation.1 | async-start | bytes 2097152 | tf_op jit(solution)/shard_map/psum | solution.py:27
  65.9 204.3 %all-gather.5.cloned.1.call-start = ((), (), s32[]{:S(2)}) async-start(), calls=%async_computation.2 | async-start | bytes 4456448 | tf_op jit(solution)/shard_map/all_gather | solution.py:23
  70.3 202.8 %copy-start.1 = (bf16[128,1024]{1,0:T(8,128)(2,1)S(1)}, bf16[128,1024]{1,0:T(8,128)(2,1)}, u32[]{:S(2)}) copy-start(bf16[128,1024]{1,0:T(8,128)(2,1)} %param.3) | copy-start | bytes 786436
  270.1 3.4 %copy-start = (bf16[2048,1024]{1,0:T(8,128)(2,1)S(1)}, bf16[2048,1024]{1,0:T(8,128)(2,1)}, u32[]{:S(2)}) copy-start(bf16[2048,1024]{1,0:T(8,128)(2,1)} %all-gather.3.cloned.1.call-done) | copy-start | bytes 12582916
Sparse Core Ops, SparseCore 0:
  9.5 51.5 all-gather.2
  66.0 153.6 all-reduce.1
  221.8 48.2 all-gather.4
where the time goes:
time: 282 us
  waiting for transfers between devices  191 us (68%)
  blocking collectives  61.8 us (22%)
  between operations  13.8 us (5%)
  matrix products  9.43 us (3%)
  other arithmetic  4.77 us (2%)
    psum x1, waiting for transfers between devices, on_device(): gram, norms = lax.psum((partial_value, squares), 'field')  87.4 us
    psum x1, blocking collectives, on_device(): gram, norms = lax.psum((partial_value, squares), 'field')  61.8 us
    all_gather x1, waiting for transfers between devices, on_device(): lax.all_gather(particles, 'dom', axis=0, tiled=True)  53.8 us
    all_gather x1, waiting for transfers between devices, on_device(): lax.all_gather(gradients, 'dom', axis=0, tiled=True)  48.7 us
  transfers between devices with their start and end apart: 3, of which 3 were waited for; matrix products, arithmetic and copies ran while one was open for 2% of the time, Pallas kernels for 0%

commit v1 on v0

v1 whole, which is shorter than its diff:
```python
import jax
import jax.numpy as jnp
from jax import lax
from jax.sharding import Mesh, PartitionSpec as P

DOM = ("z", "core")
FIELD = ("y", "x")
NF = 32


def dot_rows(left, right):
    return lax.dot_general(
        left, right, (((1,), (1,)), ((), ())), preferred_element_type=jnp.float32
    )


def squares_of(block):
    wide = block.astype(jnp.float32)
    return jnp.sum(wide * wide, axis=1)


def on_device(particles, gradients, kernel_scale):
    scale = kernel_scale[0]
    all_coords = lax.all_gather(particles, DOM, axis=0, tiled=True)
    all_grads = lax.all_gather(gradients, DOM, axis=0, tiled=True)
    partial = (
        squares_of(particles)[:, None]
        + squares_of(all_coords)[None, :]
        - 2.0 * dot_rows(particles, all_coords)
    ).astype(jnp.bfloat16)
    slots = partial.reshape(2, 64, 16, 128).transpose(2, 0, 1, 3).reshape(NF, 64, 128)
    terms = lax.all_to_all(slots, FIELD, 0, 0, tiled=True)
    dist = jnp.maximum(jnp.sum(terms.astype(jnp.float32), axis=0), 0.0)
    piece = jnp.exp(-dist / scale).astype(jnp.bfloat16)
    pieces = lax.all_to_all(
        jnp.broadcast_to(piece[None], (NF, 64, 128)), FIELD, 0, 0, tiled=True
    )
    kernel = pieces.reshape(16, 2, 64, 128).transpose(1, 2, 0, 3).reshape(128, 2048)
    weight = jnp.sum(kernel.astype(jnp.float32), axis=1)
    pulled = jnp.dot(kernel, all_grads, preferred_element_type=jnp.float32)
    spread = jnp.dot(kernel, all_coords, preferred_element_type=jnp.float32)
    coords = particles.astype(jnp.float32)
    return (0.5 * scale * pulled - spread + weight[:, None] * coords) / weight[:, None]


def solution(mesh):
    fine = Mesh(mesh.devices.reshape(8, 2, 8, 4), DOM + FIELD)
    placed = (P(DOM, FIELD), P(DOM, FIELD), P())
    return jax.shard_map(
        on_device, mesh=fine, in_specs=placed, out_specs=P(DOM, FIELD), check_vma=False
    )
```

time: 282 us -> 129 us (0.46)
  the two profiles are of different devices: /device:TPU:1 before, /device:TPU:8 now
where the time goes in v1:
time: 129 us; the launch traced here: 128 us
  waiting for transfers between devices  85.5 us (66%)
  starting transfers between devices  15.1 us (12%)
  between operations  14.1 us (11%)
  matrix products  6.21 us (5%)
  other arithmetic  4.57 us (4%)
  local copies, waits for them, and re-layouts  2.98 us (2%)
    all_gather x1, waiting for transfers between devices, on_device(): all_coords = lax.all_gather(particles, DOM, axis=0, tiled=True)  50.7 us
    all_to_all x1, waiting for transfers between devices, on_device(): terms = lax.all_to_all(slots, FIELD, 0, 0, tiled=True)  17 us
    all_to_all x1, waiting for transfers between devices, on_device(): lax.all_to_all(jnp.broadcast_to(piece[None], (NF, 64, 128)), FIELD, 0, 0,...  16.4 us
    all_to_all x1, starting transfers between devices, on_device(): terms = lax.all_to_all(slots, FIELD, 0, 0, tiled=True)  9.85 us
    all_to_all x1, starting transfers between devices, on_device(): lax.all_to_all(jnp.broadcast_to(piece[None], (NF, 64, 128)), FIELD, 0, 0,...  5.2 us
    reduce_sum x2, other arithmetic, squares_of(): return jnp.sum(wide * wide, axis=1)  4.31 us
    dot_general x1, matrix products, on_device(): pulled = jnp.dot(kernel, all_grads, preferred_element_type=jnp.float32)  3.07 us
  transfers between devices with their start and end apart: 4, of which 3 were waited for; matrix products, arithmetic and copies ran while one was open for 7% of the time, Pallas kernels for 0%

profile of v1, /device:TPU:8, one launch (start us, length us, event | category | flops | bytes accessed | tf_op | source)
XLA Modules:
  0.0 128.4 jit_solution(17678697973361711020)
XLA Ops:
  6.5 0.0 copy-start.2
  6.5 0.0 all-gather.3.cloned.1.call-start
  6.5 0.7 all-gather.3.cloned.1.call-update
  7.3 0.0 all-gather.5.cloned.1.call-start
  7.3 0.7 all-gather.5.cloned.1.call-update
  8.0 1.1 fusion.5
  9.1 50.7 %all-gather.3.cloned.1.call-done = bf16[2048,1024]{1,0:T(8,128)(2,1)} async-done(((bf16[128,1024]{1,0:T(8,128)(2,1)}), bf16[2048,1024]{1,0:T(8,128)(2,1)}) %all-gather.3.cloned.1.call-update) | async-done | bytes 4194320 | tf_op jit(solution)/shard_map/all_gather | solution.py:24
  59.8 0.0 copy-start
  59.8 3.2 %multiply_reduce_fusion = f32[2048]{0:T(1024)S(1)} fusion(bf16[2048,1024]{1,0:T(8,128)(2,1)} %all-gather.3.cloned.1.call-done), kind=kLoop, calls=%fused_computation | loop fusion | flops 6289408 | bytes 4202496 | tf_op jit(solution)/shard_map/reduce_sum | solution.py:19
  63.0 0.0 copy-done.2
  63.0 0.2 copy-done
  63.2 1.5 %fusion.2 = bf16[16,8,16,128]{3,1,2,0:T(8,128)(2,1)S(1)} fusion(bf16[128,1024]{1,0:T(8,128)(2,1)S(1)} %copy-done.2, bf16[2048,1024]{1,0:T(8,128)(2,1)S(1)} %copy-done, f32[2048]{0:T(1024)S(1)} %multiply_reduce_fusion, f32[128]{0:T(128)S(1)} %fusion.5), kind=kOutput, calls=%fused_computation.6 | convolution fusion | flops 537919488 | bytes 4989440 | tf_op jit(solution)/shard_map/dot_general | solution.py:12
  64.7 0.1 copy.7
  64.9 0.9 copy.5
  65.8 9.8 %all-to-all-start = ((bf16[32,64,128]{2,1,0:T(8,128)(2,1)}), bf16[32,64,128]{2,1,0:T(8,128)(2,1)S(1)}, u32[]{:S(2)}, u32[]{:S(2)}) async-start(bf16[32,64,128]{2,1,0:T(8,128)(2,1)} %bitcast.2), calls=%async_computation | async-start | bytes 1048576 | tf_op jit(solution)/shard_map/all_to_all | solution.py:32
  76.3 17.0 %all-to-all-done = bf16[32,64,128]{2,1,0:T(8,128)(2,1)S(1)} async-done(((bf16[32,64,128]{2,1,0:T(8,128)(2,1)}), bf16[32,64,128]{2,1,0:T(8,128)(2,1)S(1)}, u32[]{:S(2)}, u32[]{:S(2)}) %all-to-all-start) | async-done | bytes 524320 | tf_op jit(solution)/shard_map/all_to_all | solution.py:32
  93.3 0.1 convert_reduce_fusion.1
  93.4 0.9 broadcast_in_dim.2
  94.3 5.2 %all-to-all-start.1 = ((bf16[32,64,128]{2,1,0:T(8,128)(2,1)}), bf16[32,64,128]{2,1,0:T(8,128)(2,1)S(1)}, u32[]{:S(2)}, u32[]{:S(2)}) async-start(bf16[32,64,128]{2,1,0:T(8,128)(2,1)} %broadcast_in_dim.2), calls=%async_computation.1 | async-start | bytes 1048576 | tf_op jit(solution)/shard_map/all_to_all | solution.py:35
  99.5 16.4 %all-to-all-done.1 = bf16[32,64,128]{2,1,0:T(8,128)(2,1)S(1)} async-done(((bf16[32,64,128]{2,1,0:T(8,128)(2,1)}), bf16[32,64,128]{2,1,0:T(8,128)(2,1)S(1)}, u32[]{:S(2)}, u32[]{:S(2)}) %all-to-all-start.1) | async-done | bytes 524320 | tf_op jit(solution)/shard_map/all_to_all | solution.py:35
  116.0 0.3 copy.6
  116.3 0.2 convert_reduce_fusion
  116.5 0.1 mul.34
  116.5 0.0 all-gather.5.cloned.1.call-done
  116.5 0.0 copy-start.1
  116.5 3.1 %convolution_multiply_fusion.1 = f32[128,1024]{1,0:T(8,128)S(1)} fusion(bf16[2048,1024]{1,0:T(8,128)(2,1)} %all-gather.5.cloned.1.call-done, bf16[16,8,16,128]{3,2,1,0:T(8,128)(2,1)S(1)} %bitcast.27, f32[]{:T(128)S(6)} %mul_shard_map.3), kind=kOutput, calls=%fused_computation.5 | convolution fusion | flops 537001984 | bytes 5242884 | tf_op jit(solution)/shard_map/dot_general | solution.py:40
  119.6 0.4 copy-done.1
  120.0 1.6 %fusion.4 = f32[128,1024]{1,0:T(8,128)} fusion(f32[128,1024]{1,0:T(8,128)S(1)} %convolution_multiply_fusion.1, bf16[2048,1024]{1,0:T(8,128)(2,1)S(1)} %copy-done.1, bf16[128,1024]{1,0:T(8,128)(2,1)S(1)} %copy-done.2, bf16[16,8,16,128]{3,2,1,0:T(8,128)(2,1)S(1)} %bitcast.28, f32[128]{0:T(128)S(1)} %mul.34), kind=kOutput, calls=%fused_computation.8 | convolution fusion | flops 537526272 | bytes 6029824 | tf_op jit(solution)/shard_map/dot_general | solution.py:41
  (1 shorter events, 0.0 us)
Async XLA Ops:
  6.5 56.5 %copy-start.2 = (bf16[128,1024]{1,0:T(8,128)(2,1)S(1)}, bf16[128,1024]{1,0:T(8,128)(2,1)}, u32[]{:S(2)}) copy-start(bf16[128,1024]{1,0:T(8,128)(2,1)} %param.3) | copy-start | bytes 786436
  6.5 53.2 %all-gather.3.cloned.1.call-start = ((), (), s32[]{:S(2)}) async-start(), calls=%async_computation.2 | async-start | bytes 4456448 | tf_op jit(solution)/shard_map/all_gather | solution.py:24
  7.3 109.3 %all-gather.5.cloned.1.call-start = ((), (), s32[]{:S(2)}) async-start(), calls=%async_computation.3 | async-start | bytes 4456448 | tf_op jit(solution)/shard_map/all_gather | solution.py:25
  59.8 3.4 %copy-start = (bf16[2048,1024]{1,0:T(8,128)(2,1)S(1)}, bf16[2048,1024]{1,0:T(8,128)(2,1)}, u32[]{:S(2)}) copy-start(bf16[2048,1024]{1,0:T(8,128)(2,1)} %all-gather.3.cloned.1.call-done) | copy-start | bytes 12582916
  65.8 27.5 %all-to-all-start = ((bf16[32,64,128]{2,1,0:T(8,128)(2,1)}), bf16[32,64,128]{2,1,0:T(8,128)(2,1)S(1)}, u32[]{:S(2)}, u32[]{:S(2)}) async-start(bf16[32,64,128]{2,1,0:T(8,128)(2,1)} %bitcast.2), calls=%async_computation | async-start | bytes 1048576 | tf_op jit(solution)/shard_map/all_to_all | solution.py:32
  94.3 21.7 %all-to-all-start.1 = ((bf16[32,64,128]{2,1,0:T(8,128)(2,1)}), bf16[32,64,128]{2,1,0:T(8,128)(2,1)S(1)}, u32[]{:S(2)}, u32[]{:S(2)}) async-start(bf16[32,64,128]{2,1,0:T(8,128)(2,1)} %broadcast_in_dim.2), calls=%async_computation.1 | async-start | bytes 1048576 | tf_op jit(solution)/shard_map/all_to_all | solution.py:35
  116.5 3.5 %copy-start.1 = (bf16[2048,1024]{1,0:T(8,128)(2,1)S(1)}, bf16[2048,1024]{1,0:T(8,128)(2,1)}, u32[]{:S(2)}) copy-start(bf16[2048,1024]{1,0:T(8,128)(2,1)} %all-gather.3.cloned.1.call-done) | copy-start | bytes 12582916
Sparse Core Ops, SparseCore 0:
  9.5 50.2 all-gather.2
  61.9 43.7 all-gather.4

commit v2 on v1

v2 whole, which is shorter than its diff:
```python
import jax
import jax.numpy as jnp
import numpy as np
from jax import lax
from jax.experimental import pallas as pl
from jax.experimental.pallas import tpu as pltpu
from jax.sharding import Mesh, PartitionSpec as P

DOM = ("z", "core")
FIELD = ("y", "x")
NZ, NC, NY, NX = 8, 2, 8, 4
NF = NY * NX
ROWS, COLS = 128, 1024
VMEM = 48 * 1024 * 1024
OFFSETS = (0, -1, -2, 2, 1, 3, 4, -3)


def dot_rows(left, right):
    return lax.dot_general(
        left, right, (((1,), (1,)), ((), ())), preferred_element_type=jnp.float32
    )


def shift(array, hops):
    return lax.ppermute(array, "z", [(i, (i + hops) % NZ) for i in range(NZ)])


def other_core(array):
    return lax.ppermute(array, "core", [(0, 1), (1, 0)])


def partial_body(a0, b0, a1, b1, a2, b2, a3, b3, out):
    blocks = [ref[...] for ref in (a0, b0, a1, b1, a2, b2, a3, b3)]
    ones = jnp.ones((ROWS, COLS), jnp.bfloat16)
    high, low = [], []
    for block in blocks:
        wide = block.astype(jnp.float32)
        square = wide * wide
        top = square.astype(jnp.bfloat16)
        high.append(top)
        low.append((square - top.astype(jnp.float32)).astype(jnp.bfloat16))

    def along_lanes(i):
        return dot_rows(ones[:8], high[i]) + dot_rows(ones[:8], low[i])

    def along_rows(i):
        return dot_rows(high[i], ones) + dot_rows(low[i], ones)

    lanes = [along_lanes(i)[0:1] for i in range(8)]
    for row, first, columns in ((0, 0, range(8)), (2, 16, (0, 1, 6, 7)), (6, 24, (4, 5, 2, 3))):
        norms = along_rows(row)
        for j, col in enumerate(columns):
            gram = dot_rows(blocks[row], blocks[col])
            part = (norms + lanes[col] - 2.0 * gram).astype(jnp.bfloat16)
            block = first + (j // 2) * 4 + j % 2
            out[block] = part[:64]
            out[block + 2] = part[64:]


def partial_distances(*blocks):
    return pl.pallas_call(
        partial_body,
        out_shape=jax.ShapeDtypeStruct((NF, 64, 128), jnp.bfloat16),
        in_specs=[pl.BlockSpec(memory_space=pltpu.VMEM)] * 8,
        out_specs=pl.BlockSpec(memory_space=pltpu.VMEM),
        compiler_params=pltpu.CompilerParams(vmem_limit_bytes=VMEM),
        cost_estimate=pl.CostEstimate(
            flops=2 * 24 * ROWS * ROWS * COLS, bytes_accessed=5 << 19, transcendentals=0
        ),
    )(*blocks)


def update_body(place, scale, slots, both, coords, out, pulled, spread, weight):
    step = pl.program_id(0)

    @pl.when(step == 0)
    def _():
        pulled[...] = jnp.zeros_like(pulled)
        spread[...] = jnp.zeros_like(spread)
        weight[...] = jnp.zeros_like(weight)

    same = jnp.concatenate([slots[0], slots[2]], axis=0)
    other = jnp.concatenate([slots[1], slots[3]], axis=0)
    swapped = place[NZ] == 1
    kernel = jnp.concatenate(
        [jnp.where(swapped, other, same), jnp.where(swapped, same, other)], axis=1
    )
    xs = jnp.concatenate([both[0, 0:128], both[0, 256:384]], axis=0)
    gs = jnp.concatenate([both[0, 128:256], both[0, 384:512]], axis=0)
    pulled[...] += jnp.dot(kernel, gs, preferred_element_type=jnp.float32)
    spread[...] += jnp.dot(kernel, xs, preferred_element_type=jnp.float32)
    weight[...] += jnp.sum(kernel.astype(jnp.float32), axis=1, keepdims=True)

    @pl.when(step == NZ - 1)
    def _():
        total = weight[...]
        out[...] = (
            (0.5 * scale[0]) * pulled[...]
            - spread[...]
            + total * coords[...].astype(jnp.float32)
        ) / total


def update(place, scale, slots, both, coords):
    return pl.pallas_call(
        update_body,
        out_shape=jax.ShapeDtypeStruct((ROWS, COLS), jnp.float32),
        grid_spec=pltpu.PrefetchScalarGridSpec(
            num_scalar_prefetch=2,
            grid=(NZ,),
            in_specs=[
                pl.BlockSpec((4, 64, 128), lambda k, place, scale: (k, 0, 0)),
                pl.BlockSpec((1, 512, COLS), lambda k, place, scale: (place[k], 0, 0)),
                pl.BlockSpec((ROWS, COLS), lambda k, place, scale: (0, 0)),
            ],
            out_specs=pl.BlockSpec((ROWS, COLS), lambda k, place, scale: (0, 0)),
            scratch_shapes=[
                pltpu.VMEM((ROWS, COLS), jnp.float32),
                pltpu.VMEM((ROWS, COLS), jnp.float32),
                pltpu.VMEM((ROWS, 1), jnp.float32),
            ],
        ),
        compiler_params=pltpu.CompilerParams(vmem_limit_bytes=VMEM),
        cost_estimate=pl.CostEstimate(
            flops=4 * ROWS * 2048 * COLS, bytes_accessed=10 << 20, transcendentals=0
        ),
    )(place, scale, slots, both, coords)


def homeward():
    pairs = []
    for z in range(NZ):
        for field in range(NF):
            hops = 0 if field < 16 else (-1 if field < 24 else 2)
            pairs.append((z * NF + field, (z + hops) % NZ * NF + field))
    return pairs


def on_device(particles, gradients, kernel_scale):
    z, core = lax.axis_index("z"), lax.axis_index("core")
    place = jnp.concatenate(
        [(z + np.array(OFFSETS, np.int32) + NZ) % NZ, core[None]]
    ).astype(jnp.int32)
    both = lax.all_gather(jnp.concatenate([particles, gradients], axis=0), DOM, axis=0, tiled=True)
    a1 = shift(particles, 1)
    a2 = shift(particles, 2)
    a3 = shift(particles, -2)
    b0 = other_core(particles)
    b1, b2, b3 = other_core(a1), other_core(a2), other_core(a3)
    slots = partial_distances(particles, b0, a1, b1, a2, b2, a3, b3)
    terms = lax.all_to_all(slots, FIELD, 0, 0, tiled=True)
    dist = jnp.maximum(jnp.sum(terms.astype(jnp.float32), axis=0), 0.0)
    piece = jnp.exp(-dist / kernel_scale[0]).astype(jnp.bfloat16)
    piece = lax.ppermute(piece, ("z",) + FIELD, homeward())
    pieces = lax.all_to_all(
        jnp.broadcast_to(piece[None], (NF, 64, 128)), FIELD, 0, 0, tiled=True
    )
    return update(place, kernel_scale, pieces, both.reshape(NZ, 512, COLS), particles)


def solution(mesh):
    fine = Mesh(mesh.devices.reshape(NZ, NC, NY, NX), DOM + FIELD)
    placed = (P(DOM, FIELD), P(DOM, FIELD), P())
    return jax.shard_map(
        on_device, mesh=fine, in_specs=placed, out_specs=P(DOM, FIELD), check_vma=False
    )
```

time: 129 us -> 133 us (1.031)
  starting transfers between devices: 15.1 us -> 46.6 us
  waiting for transfers between devices: 85.5 us -> 54.4 us
  Pallas kernels: 0 us -> 11.9 us
  matrix products: 6.21 us -> 0 us
  other arithmetic: 4.57 us -> 2.73 us
    all_gather x2 -> x1, waiting for transfers between devices: 50.7 us -> 0.01 us  [on_device(): lax.all_gather(jnp.concatenate([particles, gradients], axis=0), DOM, axis...]
    ppermute x0 -> x8, starting transfers between devices: none -> 24.6 us  [the longest x3 16.2 us: shift(): return lax.ppermute(array, 'z', [(i, (i + hops) % NZ) for i in range(NZ)])]
    ppermute x0 -> x8, waiting for transfers between devices: none -> 22.3 us  [the longest x3 20.9 us: shift(): return lax.ppermute(array, 'z', [(i, (i + hops) % NZ) for i in range(NZ)])]
    pallas_call x0 -> x2, Pallas kernels: none -> 11.9 us  [the longest x1 8.31 us: update(): pl.pallas_call(update_body, out_shape=jax.ShapeDtypeStruct((ROWS, COLS),...]
    all_to_all x1, starting transfers between devices: 5.2 us -> 11.7 us  [on_device(): lax.all_to_all(jnp.broadcast_to(piece[None], (NF, 64, 128)), FIELD, 0, 0,...]
    dot_general x3 -> x0, matrix products: 6.21 us -> none  [the longest x1 3.07 us: on_device(): pulled = jnp.dot(kernel, all_grads, preferred_element_type=jnp.float32)]
    reduce_sum x3 -> x0, other arithmetic: 4.46 us -> none  [the longest x2 4.31 us: squares_of(): return jnp.sum(wide * wide, axis=1)]
    concatenate x0 -> x2, other arithmetic: none -> 1.96 us  [the longest x1 1.88 us: on_device(): jnp.concatenate([particles, gradients], axis=0)]
  transfers between devices with their start and end apart: 4 -> 11, of which waited for: 3 -> 6; matrix products, arithmetic and copies ran while one was open for 7% -> 1% of each run, Pallas kernels for 0% -> 3%
where the time goes in v2:
time: 133 us
  waiting for transfers between devices  54.4 us (41%)
  starting transfers between devices  46.6 us (35%)
  between operations  14.2 us (11%)
  Pallas kernels  11.9 us (9%)
  local copies, waits for them, and re-layouts  2.82 us (2%)
  other arithmetic  2.73 us (2%)
    ppermute x3, waiting for transfers between devices, shift(): return lax.ppermute(array, 'z', [(i, (i + hops) % NZ) for i in range(NZ)])  20.9 us
    all_to_all x1, waiting for transfers between devices, on_device(): terms = lax.all_to_all(slots, FIELD, 0, 0, tiled=True)  16.8 us
    ppermute x3, starting transfers between devices, shift(): return lax.ppermute(array, 'z', [(i, (i + hops) % NZ) for i in range(NZ)])  16.2 us
    all_to_all x1, waiting for transfers between devices, on_device(): lax.all_to_all(jnp.broadcast_to(piece[None], (NF, 64, 128)), FIELD, 0, 0,...  15.2 us
    all_to_all x1, starting transfers between devices, on_device(): lax.all_to_all(jnp.broadcast_to(piece[None], (NF, 64, 128)), FIELD, 0, 0,...  11.7 us
    all_to_all x1, starting transfers between devices, on_device(): terms = lax.all_to_all(slots, FIELD, 0, 0, tiled=True)  10.4 us
    pallas_call x1, Pallas kernels, update(): pl.pallas_call(update_body, out_shape=jax.ShapeDtypeStruct((ROWS, COLS),...  8.31 us
    ppermute x4, starting transfers between devices, other_core(): return lax.ppermute(array, 'core', [(0, 1), (1, 0)])  7.65 us
  transfers between devices with their start and end apart: 11, of which 6 were waited for; matrix products, arithmetic and copies ran while one was open for 1% of the time, Pallas kernels for 3%

profile of v2, /device:TPU:8, one launch (start us, length us, event | category | flops | bytes accessed | tf_op | source)
XLA Modules:
  0.0 132.7 jit_solution(6333801949559628858)
XLA Ops:
  6.5 0.0 all-gather.2.cloned.1.call-start
  6.5 1.9 %pad_maximum_fusion = bf16[256,1024]{1,0:T(8,128)(2,1)} fusion(bf16[128,1024]{1,0:T(8,128)(2,1)} %param.5, bf16[128,1024]{1,0:T(8,128)(2,1)} %coords.1), kind=kLoop, calls=%fused_computation.1 | loop fusion | flops 1048576 | bytes 1048576 | tf_op jit(solution)/shard_map/concatenate | solution.py:144
  8.4 0.0 all-gather.2.cloned.1.call-update
  8.4 10.9 %collective-permute-start.5 = (bf16[128,1024]{1,0:T(8,128)(2,1)}, bf16[128,1024]{1,0:T(8,128)(2,1)S(1)}, u32[]{:S(2)}, u32[]{:S(2)}) collective-permute-start(bf16[128,1024]{1,0:T(8,128)(2,1)} %coords.1), channel_id=1, source_target_pairs={{0,384},{64,448},{128,0},{192,64},{256,128},{320,192},{384,256},{4... | collective-permute-start | bytes 786440 | tf_op jit(solution)/shard_map/ppermute | solution.py:25
  19.4 1.9 %collective-permute-start.3 = (bf16[128,1024]{1,0:T(8,128)(2,1)}, bf16[128,1024]{1,0:T(8,128)(2,1)S(1)}, u32[]{:S(2)}, u32[]{:S(2)}) collective-permute-start(bf16[128,1024]{1,0:T(8,128)(2,1)} %coords.1), channel_id=1, source_target_pairs={{0,128},{64,192},{128,256},{192,320},{256,384},{320,448},{384,0},{... | collective-permute-start | bytes 786440 | tf_op jit(solution)/shard_map/ppermute | solution.py:25
  21.3 3.4 %collective-permute-start.1 = (bf16[128,1024]{1,0:T(8,128)(2,1)}, bf16[128,1024]{1,0:T(8,128)(2,1)S(1)}, u32[]{:S(2)}, u32[]{:S(2)}) collective-permute-start(bf16[128,1024]{1,0:T(8,128)(2,1)} %coords.1), channel_id=1, source_target_pairs={{0,64},{64,128},{128,192},{192,256},{256,320},{320,384},{384,448},... | collective-permute-start | bytes 786440 | tf_op jit(solution)/shard_map/ppermute | solution.py:25
  24.7 1.9 %collective-permute-start = (bf16[128,1024]{1,0:T(8,128)(2,1)}, bf16[128,1024]{1,0:T(8,128)(2,1)S(1)}, u32[]{:S(2)}, u32[]{:S(2)}) collective-permute-start(bf16[128,1024]{1,0:T(8,128)(2,1)} %coords.1), channel_id=1, source_target_pairs={{0,32},{32,0},{1,33},{33,1},{2,34},{34,2},{3,35},{35,3},{4,36},{36... | collective-permute-start | bytes 786440 | tf_op jit(solution)/shard_map/ppermute | solution.py:29
  26.6 7.0 %collective-permute-done.5.a3 = bf16[128,1024]{1,0:T(8,128)(2,1)S(1)} collective-permute-done((bf16[128,1024]{1,0:T(8,128)(2,1)}, bf16[128,1024]{1,0:T(8,128)(2,1)S(1)}, u32[]{:S(2)}, u32[]{:S(2)}) %collective-permute-start.5) | collective-permute-done | bytes 262176 | tf_op jit(solution)/shard_map/ppermute | solution.py:25
  33.7 1.9 %collective-permute-start.6 = (bf16[128,1024]{1,0:T(8,128)(2,1)S(1)}, bf16[128,1024]{1,0:T(8,128)(2,1)S(1)}, u32[]{:S(2)}, u32[]{:S(2)}) collective-permute-start(bf16[128,1024]{1,0:T(8,128)(2,1)S(1)} %collective-permute-done.5.a3), channel_id=1, source_target_pairs={{0,32},{32,0},{1,33},{33,1},{2,34},{34,2},{3,35},{35,3},{4,36},{36... | collective-permute-start | bytes 786440 | tf_op jit(solution)/shard_map/ppermute | solution.py:29
  35.6 5.6 %collective-permute-done.3.a2 = bf16[128,1024]{1,0:T(8,128)(2,1)S(1)} collective-permute-done((bf16[128,1024]{1,0:T(8,128)(2,1)}, bf16[128,1024]{1,0:T(8,128)(2,1)S(1)}, u32[]{:S(2)}, u32[]{:S(2)}) %collective-permute-start.3) | collective-permute-done | bytes 262176 | tf_op jit(solution)/shard_map/ppermute | solution.py:25
  41.2 1.9 %collective-permute-start.4 = (bf16[128,1024]{1,0:T(8,128)(2,1)S(1)}, bf16[128,1024]{1,0:T(8,128)(2,1)S(1)}, u32[]{:S(2)}, u32[]{:S(2)}) collective-permute-start(bf16[128,1024]{1,0:T(8,128)(2,1)S(1)} %collective-permute-done.3.a2), channel_id=1, source_target_pairs={{0,32},{32,0},{1,33},{33,1},{2,34},{34,2},{3,35},{35,3},{4,36},{36... | collective-permute-start | bytes 786440 | tf_op jit(solution)/shard_map/ppermute | solution.py:29
  43.1 8.3 %collective-permute-done.1.a1 = bf16[128,1024]{1,0:T(8,128)(2,1)S(1)} collective-permute-done((bf16[128,1024]{1,0:T(8,128)(2,1)}, bf16[128,1024]{1,0:T(8,128)(2,1)S(1)}, u32[]{:S(2)}, u32[]{:S(2)}) %collective-permute-start.1) | collective-permute-done | bytes 262176 | tf_op jit(solution)/shard_map/ppermute | solution.py:25
  51.3 1.9 %collective-permute-start.2 = (bf16[128,1024]{1,0:T(8,128)(2,1)S(1)}, bf16[128,1024]{1,0:T(8,128)(2,1)S(1)}, u32[]{:S(2)}, u32[]{:S(2)}) collective-permute-start(bf16[128,1024]{1,0:T(8,128)(2,1)S(1)} %collective-permute-done.1.a1), channel_id=1, source_target_pairs={{0,32},{32,0},{1,33},{33,1},{2,34},{34,2},{3,35},{35,3},{4,36},{36... | collective-permute-start | bytes 786440 | tf_op jit(solution)/shard_map/ppermute | solution.py:29
  53.3 0.0 collective-permute-done.b0
  53.3 0.0 collective-permute-done.6.b3
  53.3 0.0 collective-permute-done.4.b2
  53.3 1.5 %collective-permute-done.2.b1 = bf16[128,1024]{1,0:T(8,128)(2,1)S(1)} collective-permute-done((bf16[128,1024]{1,0:T(8,128)(2,1)S(1)}, bf16[128,1024]{1,0:T(8,128)(2,1)S(1)}, u32[]{:S(2)}, u32[]{:S(2)}) %collective-permute-start.2) | collective-permute-done | bytes 262176 | tf_op jit(solution)/shard_map/ppermute | solution.py:29
  54.8 0.0 copy-start
  54.8 1.0 copy-done
  55.7 3.6 %shard_map.46 = bf16[32,64,128]{2,1,0:T(8,128)(2,1)} custom-call(bf16[128,1024]{1,0:T(8,128)(2,1)S(1)} %copy-done, bf16[128,1024]{1,0:T(8,128)(2,1)S(1)} %collective-permute-done.b0, bf16[128,1024]{1,0:T(8,128)(2,1)S(1)} %collective-permute-done.1.a1, bf16[128,1024]{1,0:T(8,128)(2,1)S(1)} %collective-permute-done.2.b1, ...), custom_call_target="tpu_custom_call" | custom-call | flops 805306368 | bytes 2621440 | tf_op jit(solution)/shard_map/pallas_call | solution.py:61
  59.3 10.4 %all-to-all-start = ((bf16[32,64,128]{2,1,0:T(8,128)(2,1)}), bf16[32,64,128]{2,1,0:T(8,128)(2,1)S(1)}, u32[]{:S(2)}, u32[]{:S(2)}) async-start(bf16[32,64,128]{2,1,0:T(8,128)(2,1)} %shard_map.46), calls=%async_computation | async-start | bytes 1048576 | tf_op jit(solution)/shard_map/all_to_all | solution.py:151
  70.4 16.8 %all-to-all-done = bf16[32,64,128]{2,1,0:T(8,128)(2,1)S(1)} async-done(((bf16[32,64,128]{2,1,0:T(8,128)(2,1)}), bf16[32,64,128]{2,1,0:T(8,128)(2,1)S(1)}, u32[]{:S(2)}, u32[]{:S(2)}) %all-to-all-start) | async-done | bytes 524320 | tf_op jit(solution)/shard_map/all_to_all | solution.py:151
  87.2 0.1 convert_reduce_fusion
  87.4 0.7 collective-permute-start.7
  88.0 0.0 collective-permute-done.7
  88.0 0.9 broadcast_in_dim.10
  88.9 11.7 %all-to-all-start.1 = ((bf16[32,64,128]{2,1,0:T(8,128)(2,1)}), bf16[32,64,128]{2,1,0:T(8,128)(2,1)S(1)}, u32[]{:S(2)}, u32[]{:S(2)}) async-start(bf16[32,64,128]{2,1,0:T(8,128)(2,1)} %broadcast_in_dim.10), calls=%async_computation.1 | async-start | bytes 1048576 | tf_op jit(solution)/shard_map/all_to_all | solution.py:155
  100.6 0.7 and_select_fusion
  101.3 0.1 pad_add_fusion.place
  101.4 15.2 %all-to-all-done.1.slots = bf16[32,64,128]{2,1,0:T(8,128)(2,1)S(1)} async-done(((bf16[32,64,128]{2,1,0:T(8,128)(2,1)}), bf16[32,64,128]{2,1,0:T(8,128)(2,1)S(1)}, u32[]{:S(2)}, u32[]{:S(2)}) %all-to-all-start.1) | async-done | bytes 524320 | tf_op jit(solution)/shard_map/all_to_all | solution.py:155
  116.6 0.0 all-gather.2.cloned.1.call-done
  116.6 0.0 copy-start.1
  116.6 0.9 copy-done.1
  117.5 8.3 %shard_map.47 = f32[128,1024]{1,0:T(8,128)} custom-call(s32[9]{0:T(128)S(1)} %pad_add_fusion.place, f32[1]{0:T(128)} %copy.5.scale, bf16[32,64,128]{2,1,0:T(8,128)(2,1)S(1)} %all-to-all-done.1.slots, bf16[8,512,1024]{2,1,0:T(8,128)(2,1)} %bitcast.4, bf16[128,1024]{1,0:T(8,128)(2,1)S(1)} %copy-done.1), custom_call_target="tpu_custom_call" | custom-call | flops 1073741824 | bytes 10485760 | tf_op jit(solution)/shard_map/pallas_call | solution.py:105
  (1 shorter events, 0.0 us)
Async XLA Ops:
  6.5 110.0 %all-gather.2.cloned.1.call-start = ((), (), s32[]{:S(2)}) async-start(), calls=%async_computation.2 | async-start | bytes 8912896 | tf_op jit(solution)/shard_map/all_gather | solution.py:144
  8.4 25.2 %collective-permute-start.5 = (bf16[128,1024]{1,0:T(8,128)(2,1)}, bf16[128,1024]{1,0:T(8,128)(2,1)S(1)}, u32[]{:S(2)}, u32[]{:S(2)}) collective-permute-start(bf16[128,1024]{1,0:T(8,128)(2,1)} %coords.1), channel_id=1, source_target_pairs={{0,384},{64,448},{128,0},{192,64},{256,128},{320,192},{384,256},{4... | collective-permute-start | bytes 786440 | tf_op jit(solution)/shard_map/ppermute | solution.py:25
  19.4 21.8 %collective-permute-start.3 = (bf16[128,1024]{1,0:T(8,128)(2,1)}, bf16[128,1024]{1,0:T(8,128)(2,1)S(1)}, u32[]{:S(2)}, u32[]{:S(2)}) collective-permute-start(bf16[128,1024]{1,0:T(8,128)(2,1)} %coords.1), channel_id=1, source_target_pairs={{0,128},{64,192},{128,256},{192,320},{256,384},{320,448},{384,0},{... | collective-permute-start | bytes 786440 | tf_op jit(solution)/shard_map/ppermute | solution.py:25
  21.3 30.0 %collective-permute-start.1 = (bf16[128,1024]{1,0:T(8,128)(2,1)}, bf16[128,1024]{1,0:T(8,128)(2,1)S(1)}, u32[]{:S(2)}, u32[]{:S(2)}) collective-permute-start(bf16[128,1024]{1,0:T(8,128)(2,1)} %coords.1), channel_id=1, source_target_pairs={{0,64},{64,128},{128,192},{192,256},{256,320},{320,384},{384,448},... | collective-permute-start | bytes 786440 | tf_op jit(solution)/shard_map/ppermute | solution.py:25
  24.7 28.5 %collective-permute-start = (bf16[128,1024]{1,0:T(8,128)(2,1)}, bf16[128,1024]{1,0:T(8,128)(2,1)S(1)}, u32[]{:S(2)}, u32[]{:S(2)}) collective-permute-start(bf16[128,1024]{1,0:T(8,128)(2,1)} %coords.1), channel_id=1, source_target_pairs={{0,32},{32,0},{1,33},{33,1},{2,34},{34,2},{3,35},{35,3},{4,36},{36... | collective-permute-start | bytes 786440 | tf_op jit(solution)/shard_map/ppermute | solution.py:29
  33.7 19.6 %collective-permute-start.6 = (bf16[128,1024]{1,0:T(8,128)(2,1)S(1)}, bf16[128,1024]{1,0:T(8,128)(2,1)S(1)}, u32[]{:S(2)}, u32[]{:S(2)}) collective-permute-start(bf16[128,1024]{1,0:T(8,128)(2,1)S(1)} %collective-permute-done.5.a3), channel_id=1, source_target_pairs={{0,32},{32,0},{1,33},{33,1},{2,34},{34,2},{3,35},{35,3},{4,36},{36... | collective-permute-start | bytes 786440 | tf_op jit(solution)/shard_map/ppermute | solution.py:29
  41.2 12.1 %collective-permute-start.4 = (bf16[128,1024]{1,0:T(8,128)(2,1)S(1)}, bf16[128,1024]{1,0:T(8,128)(2,1)S(1)}, u32[]{:S(2)}, u32[]{:S(2)}) collective-permute-start(bf16[128,1024]{1,0:T(8,128)(2,1)S(1)} %collective-permute-done.3.a2), channel_id=1, source_target_pairs={{0,32},{32,0},{1,33},{33,1},{2,34},{34,2},{3,35},{35,3},{4,36},{36... | collective-permute-start | bytes 786440 | tf_op jit(solution)/shard_map/ppermute | solution.py:29
  51.3 3.4 %collective-permute-start.2 = (bf16[128,1024]{1,0:T(8,128)(2,1)S(1)}, bf16[128,1024]{1,0:T(8,128)(2,1)S(1)}, u32[]{:S(2)}, u32[]{:S(2)}) collective-permute-start(bf16[128,1024]{1,0:T(8,128)(2,1)S(1)} %collective-permute-done.1.a1), channel_id=1, source_target_pairs={{0,32},{32,0},{1,33},{33,1},{2,34},{34,2},{3,35},{35,3},{4,36},{36... | collective-permute-start | bytes 786440 | tf_op jit(solution)/shard_map/ppermute | solution.py:29
  54.8 1.0 copy-start
  59.3 27.9 %all-to-all-start = ((bf16[32,64,128]{2,1,0:T(8,128)(2,1)}), bf16[32,64,128]{2,1,0:T(8,128)(2,1)S(1)}, u32[]{:S(2)}, u32[]{:S(2)}) async-start(bf16[32,64,128]{2,1,0:T(8,128)(2,1)} %shard_map.46), calls=%async_computation | async-start | bytes 1048576 | tf_op jit(solution)/shard_map/all_to_all | solution.py:151
  87.4 0.7 collective-permute-start.7
  88.9 27.6 %all-to-all-start.1 = ((bf16[32,64,128]{2,1,0:T(8,128)(2,1)}), bf16[32,64,128]{2,1,0:T(8,128)(2,1)S(1)}, u32[]{:S(2)}, u32[]{:S(2)}) async-start(bf16[32,64,128]{2,1,0:T(8,128)(2,1)} %broadcast_in_dim.10), calls=%async_computation.1 | async-start | bytes 1048576 | tf_op jit(solution)/shard_map/all_to_all | solution.py:155
  116.6 1.0 copy-start.1
Sparse Core Ops, SparseCore 0:
  9.5 74.1 all-gather.1

commit v3 on v2

v3 whole, which is shorter than its diff:
```python
import jax
import jax.numpy as jnp
import numpy as np
from jax import lax
from jax.experimental import pallas as pl
from jax.experimental.pallas import tpu as pltpu
from jax.sharding import Mesh, PartitionSpec as P

DOM = ("z", "core")
FIELD = ("y", "x")
NZ, NC, NY, NX = 8, 2, 8, 4
NF = NY * NX
ROWS, COLS = 128, 1024
VMEM = 48 * 1024 * 1024
OFFSETS = (0, -1, -2, 2, 1, 3, 4, -3)


def dot_rows(left, right):
    return lax.dot_general(
        left, right, (((1,), (1,)), ((), ())), preferred_element_type=jnp.float32
    )


def shift(array, hops):
    return lax.ppermute(array, "z", [(i, (i + hops) % NZ) for i in range(NZ)])


def other_core(array):
    return lax.ppermute(array, "core", [(0, 1), (1, 0)])


def partial_body(source, b0, a1, b1, far, far_b, out, a0, arrived):
    copy = pltpu.make_async_copy(source, a0, arrived)
    copy.start()
    copy.wait()
    blocks = [ref[...] for ref in (a0, b0, a1, b1)]
    blocks += [far[:ROWS], far_b[:ROWS], far[ROWS:], far_b[ROWS:]]
    ones = jnp.ones((ROWS, COLS), jnp.bfloat16)
    high, low = [], []
    for block in blocks:
        wide = block.astype(jnp.float32)
        square = wide * wide
        top = square.astype(jnp.bfloat16)
        high.append(top)
        low.append((square - top.astype(jnp.float32)).astype(jnp.bfloat16))

    def along_lanes(i):
        return dot_rows(ones[:8], high[i]) + dot_rows(ones[:8], low[i])

    def along_rows(i):
        return dot_rows(high[i], ones) + dot_rows(low[i], ones)

    lanes = [along_lanes(i)[0:1] for i in range(8)]
    for row, first, columns in ((0, 0, range(8)), (2, 16, (0, 1, 6, 7)), (6, 24, (4, 5, 2, 3))):
        norms = along_rows(row)
        for j, col in enumerate(columns):
            gram = dot_rows(blocks[row], blocks[col])
            part = (norms + lanes[col] - 2.0 * gram).astype(jnp.bfloat16)
            block = first + (j // 2) * 4 + j % 2
            out[block] = part[:64]
            out[block + 2] = part[64:]


def partial_distances(*blocks):
    return pl.pallas_call(
        partial_body,
        out_shape=jax.ShapeDtypeStruct((NF, 64, 128), jnp.bfloat16),
        in_specs=[pl.BlockSpec(memory_space=pltpu.HBM)]
        + [pl.BlockSpec(memory_space=pltpu.VMEM)] * 5,
        out_specs=pl.BlockSpec(memory_space=pltpu.VMEM),
        scratch_shapes=[pltpu.VMEM((ROWS, COLS), jnp.bfloat16), pltpu.SemaphoreType.DMA],
        compiler_params=pltpu.CompilerParams(vmem_limit_bytes=VMEM),
        cost_estimate=pl.CostEstimate(
            flops=2 * 24 * ROWS * ROWS * COLS, bytes_accessed=5 << 19, transcendentals=0
        ),
    )(*blocks)


def update_body(place, half, slots, both, out, kernel, weight):
    core = place[NZ]

    @pl.when(pl.program_id(0) == 0)
    def _():
        total = jnp.zeros((ROWS, 1), jnp.float32)
        for k in range(NZ):
            same = jnp.concatenate([slots[4 * k], slots[4 * k + 2]], axis=0)
            other = jnp.concatenate([slots[4 * k + 1], slots[4 * k + 3]], axis=0)
            pair = jnp.concatenate(
                [jnp.where(core == 1, other, same), jnp.where(core == 1, same, other)], axis=1
            )
            kernel[:, pl.ds(pl.multiple_of(place[k] * 256, 256), 256)] = pair
            total += jnp.sum(pair.astype(jnp.float32), axis=1, keepdims=True)
        weight[...] = total

    coords = jnp.concatenate([both[2 * d] for d in range(NZ * NC)], axis=0)
    grads = jnp.concatenate([both[2 * d + 1] for d in range(NZ * NC)], axis=0)
    pulled = jnp.dot(kernel[...], grads, preferred_element_type=jnp.float32)
    spread = jnp.dot(kernel[...], coords, preferred_element_type=jnp.float32)
    own = both[4 * place[0] + 2 * core].astype(jnp.float32)
    total = weight[...]
    out[...] = (half[0] * pulled - spread + total * own) / total


def update(place, half, slots, both):
    tile = 256
    return pl.pallas_call(
        update_body,
        out_shape=jax.ShapeDtypeStruct((ROWS, COLS), jnp.float32),
        grid_spec=pltpu.PrefetchScalarGridSpec(
            num_scalar_prefetch=2,
            grid=(COLS // tile,),
            in_specs=[
                pl.BlockSpec((NF, 64, 128), lambda k, place, half: (0, 0, 0)),
                pl.BlockSpec((2 * NZ * NC, ROWS, tile), lambda k, place, half: (0, 0, k)),
            ],
            out_specs=pl.BlockSpec((ROWS, tile), lambda k, place, half: (0, k)),
            scratch_shapes=[
                pltpu.VMEM((ROWS, 2048), jnp.bfloat16),
                pltpu.VMEM((ROWS, 1), jnp.float32),
            ],
        ),
        compiler_params=pltpu.CompilerParams(vmem_limit_bytes=VMEM),
        cost_estimate=pl.CostEstimate(
            flops=4 * ROWS * 2048 * COLS, bytes_accessed=10 << 20, transcendentals=0
        ),
    )(place, half, slots, both)


def homeward():
    pairs = []
    for z in range(NZ):
        for field in range(NF):
            hops = 0 if field < 16 else (-1 if field < 24 else 2)
            pairs.append((z * NF + field, (z + hops) % NZ * NF + field))
    return pairs


def on_device(particles, gradients, kernel_scale):
    z, core = lax.axis_index("z"), lax.axis_index("core")
    place = jnp.concatenate(
        [(z + np.array(OFFSETS, np.int32) + NZ) % NZ, core[None]]
    ).astype(jnp.int32)
    half = 0.5 * kernel_scale
    a1, a3 = shift(particles, 1), shift(particles, -2)
    b0 = other_core(particles)
    a1, b0 = lax.optimization_barrier((a1, b0))
    a2 = shift(a1, 1)
    b1 = other_core(a1)
    far = jnp.concatenate([a2, a3], axis=0)
    own = jnp.concatenate([particles, gradients], axis=0)
    own, far = lax.optimization_barrier((own, far))
    both = lax.all_gather(own, DOM, axis=0, tiled=True)
    slots = partial_distances(particles, b0, a1, b1, far, other_core(far))
    slots, place, half, whole = lax.optimization_barrier((slots, place, half, 2.0 * half))
    terms = lax.all_to_all(slots, FIELD, 0, 0, tiled=True)
    dist = jnp.maximum(jnp.sum(terms.astype(jnp.float32), axis=0), 0.0)
    piece = jnp.exp(-dist / whole[0]).astype(jnp.bfloat16)
    piece = lax.ppermute(piece, ("z",) + FIELD, homeward())
    pieces = lax.all_to_all(
        jnp.broadcast_to(piece[None], (NF, 64, 128)), FIELD, 0, 0, tiled=True
    )
    return update(place, half, pieces, both.reshape(2 * NZ * NC, ROWS, COLS))


def solution(mesh):
    fine = Mesh(mesh.devices.reshape(NZ, NC, NY, NX), DOM + FIELD)
    placed = (P(DOM, FIELD), P(DOM, FIELD), P())
    return jax.shard_map(
        on_device, mesh=fine, in_specs=placed, out_specs=P(DOM, FIELD), check_vma=False
    )
```

time: 133 us -> 115 us (0.86)
  blocking collectives: 0 us -> 55.8 us
  waiting for transfers between devices: 54.4 us -> 8.42 us
  starting transfers between devices: 46.6 us -> 23.1 us
  Pallas kernels: 11.9 us -> 9.22 us
  local copies, waits for them, and re-layouts: 2.82 us -> 1.06 us
    all_to_all x0 -> x2, blocking collectives: none -> 55.8 us  [the longest x1 28.2 us: on_device(): lax.all_to_all(jnp.broadcast_to(piece[None], (NF, 64, 128)), FIELD, 0, 0,...]
    all_to_all x2 -> x0, waiting for transfers between devices: 32 us -> none  [the longest x1 16.8 us: on_device(): terms = lax.all_to_all(slots, FIELD, 0, 0, tiled=True)]
    all_to_all x2 -> x0, starting transfers between devices: 22.1 us -> none  [the longest x1 11.7 us: on_device(): lax.all_to_all(jnp.broadcast_to(piece[None], (NF, 64, 128)), FIELD, 0, 0,...]
    ppermute x3, waiting for transfers between devices: 20.9 us -> 8 us  [shift(): return lax.ppermute(array, 'z', [(i, (i + hops) % NZ) for i in range(NZ)])]
    pallas_call x1, Pallas kernels: 8.31 us -> 6.38 us  [update(): pl.pallas_call(update_body, out_shape=jax.ShapeDtypeStruct((ROWS, COLS),...]
    ppermute x4 -> x3, starting transfers between devices: 7.65 us -> 6.25 us  [other_core(): return lax.ppermute(array, 'core', [(0, 1), (1, 0)])]
  transfers between devices with their start and end apart: 11 -> 8, of which waited for: 6 -> 4; matrix products, arithmetic and copies ran while one was open for 1% -> 2% of each run, Pallas kernels for 3% -> 2%
where the time goes in v3:
time: 115 us
  blocking collectives  55.8 us (49%)
  starting transfers between devices  23.1 us (20%)
  between operations  14.1 us (12%)
  Pallas kernels  9.22 us (8%)
  waiting for transfers between devices  8.42 us (7%)
  other arithmetic  2.74 us (2%)
    all_to_all x1, blocking collectives, on_device(): lax.all_to_all(jnp.broadcast_to(piece[None], (NF, 64, 128)), FIELD, 0, 0,...  28.2 us
    all_to_all x1, blocking collectives, on_device(): terms = lax.all_to_all(slots, FIELD, 0, 0, tiled=True)  27.6 us
    ppermute x3, starting transfers between devices, shift(): return lax.ppermute(array, 'z', [(i, (i + hops) % NZ) for i in range(NZ)])  16.2 us
    ppermute x3, waiting for transfers between devices, shift(): return lax.ppermute(array, 'z', [(i, (i + hops) % NZ) for i in range(NZ)])  8 us
    pallas_call x1, Pallas kernels, update(): pl.pallas_call(update_body, out_shape=jax.ShapeDtypeStruct((ROWS, COLS),...  6.38 us
    ppermute x3, starting transfers between devices, other_core(): return lax.ppermute(array, 'core', [(0, 1), (1, 0)])  6.25 us
    pallas_call x1, Pallas kernels, partial_distances(): pl.pallas_call(partial_body, out_shape=jax.ShapeDtypeStruct((NF, 64, 128)...  2.84 us
  transfers between devices with their start and end apart: 8, of which 4 were waited for; matrix products, arithmetic and copies ran while one was open for 2% of the time, Pallas kernels for 2%

profile of v3, /device:TPU:8, one launch (start us, length us, event | category | flops | bytes accessed | tf_op | source)
XLA Modules:
  0.0 114.5 jit_solution(16309411329913434709)
XLA Ops:
  6.5 0.0 all-gather.2.cloned.1.call-start
  6.5 4.3 %collective-permute-start = (bf16[128,1024]{1,0:T(8,128)(2,1)}, bf16[128,1024]{1,0:T(8,128)(2,1)S(1)}, u32[]{:S(2)}, u32[]{:S(2)}) collective-permute-start(bf16[128,1024]{1,0:T(8,128)(2,1)} %source.1), channel_id=1, source_target_pairs={{0,64},{64,128},{128,192},{192,256},{256,320},{320,384},{384,448},... | collective-permute-start | bytes 786440 | tf_op jit(solution)/shard_map/ppermute | solution.py:25
  10.8 1.9 %collective-permute-start.1 = (bf16[128,1024]{1,0:T(8,128)(2,1)}, bf16[128,1024]{1,0:T(8,128)(2,1)S(1)}, u32[]{:S(2)}, u32[]{:S(2)}) collective-permute-start(bf16[128,1024]{1,0:T(8,128)(2,1)} %source.1), channel_id=1, source_target_pairs={{0,32},{32,0},{1,33},{33,1},{2,34},{34,2},{3,35},{35,3},{4,36},{36... | collective-permute-start | bytes 786440 | tf_op jit(solution)/shard_map/ppermute | solution.py:29
  12.7 10.0 %collective-permute-start.4 = (bf16[128,1024]{1,0:T(8,128)(2,1)}, bf16[128,1024]{1,0:T(8,128)(2,1)S(1)}, u32[]{:S(2)}, u32[]{:S(2)}) collective-permute-start(bf16[128,1024]{1,0:T(8,128)(2,1)} %source.1), channel_id=1, source_target_pairs={{0,384},{64,448},{128,0},{192,64},{256,128},{320,192},{384,256},{4... | collective-permute-start | bytes 786440 | tf_op jit(solution)/shard_map/ppermute | solution.py:25
  22.8 1.2 %collective-permute-done.a1 = bf16[128,1024]{1,0:T(8,128)(2,1)S(1)} collective-permute-done((bf16[128,1024]{1,0:T(8,128)(2,1)}, bf16[128,1024]{1,0:T(8,128)(2,1)S(1)}, u32[]{:S(2)}, u32[]{:S(2)}) %collective-permute-start) | collective-permute-done | bytes 262176 | tf_op jit(solution)/shard_map/ppermute | solution.py:25
  24.0 0.0 collective-permute-done.1.b0
  24.0 1.9 %collective-permute-start.3 = (bf16[128,1024]{1,0:T(8,128)(2,1)S(1)}, bf16[128,1024]{1,0:T(8,128)(2,1)S(1)}, u32[]{:S(2)}, u32[]{:S(2)}) collective-permute-start(bf16[128,1024]{1,0:T(8,128)(2,1)S(1)} %collective-permute-done.a1), channel_id=1, source_target_pairs={{0,64},{64,128},{128,192},{192,256},{256,320},{320,384},{384,448},... | collective-permute-start | bytes 786440 | tf_op jit(solution)/shard_map/ppermute | solution.py:25
  25.9 1.9 %pad_maximum_fusion = bf16[256,1024]{1,0:T(8,128)(2,1)} fusion(bf16[128,1024]{1,0:T(8,128)(2,1)} %param.5, bf16[128,1024]{1,0:T(8,128)(2,1)} %source.1), kind=kLoop, calls=%fused_computation.1 | loop fusion | flops 1048576 | bytes 1048576 | tf_op jit(solution)/shard_map/concatenate | solution.py:150
  27.8 6.7 %collective-permute-done.4 = bf16[128,1024]{1,0:T(8,128)(2,1)S(1)} collective-permute-done((bf16[128,1024]{1,0:T(8,128)(2,1)}, bf16[128,1024]{1,0:T(8,128)(2,1)S(1)}, u32[]{:S(2)}, u32[]{:S(2)}) %collective-permute-start.4) | collective-permute-done | bytes 262176 | tf_op jit(solution)/shard_map/ppermute | solution.py:25
  34.4 0.1 collective-permute-done.3
  34.6 0.0 all-gather.2.cloned.1.call-update
  34.6 1.9 %collective-permute-start.5 = (bf16[256,1024]{1,0:T(8,128)(2,1)S(1)}, bf16[256,1024]{1,0:T(8,128)(2,1)S(1)}, u32[]{:S(2)}, u32[]{:S(2)}) collective-permute-start(bf16[256,1024]{1,0:T(8,128)(2,1)S(1)} %pad_maximum_fusion.1.far), channel_id=1, source_target_pairs={{0,32},{32,0},{1,33},{33,1},{2,34},{34,2},{3,35},{35,3},{4,36},{36... | collective-permute-start | bytes 1572872 | tf_op jit(solution)/shard_map/ppermute | solution.py:29
  37.2 2.4 %collective-permute-start.2 = (bf16[128,1024]{1,0:T(8,128)(2,1)S(1)}, bf16[128,1024]{1,0:T(8,128)(2,1)S(1)}, u32[]{:S(2)}, u32[]{:S(2)}) collective-permute-start(bf16[128,1024]{1,0:T(8,128)(2,1)S(1)} %collective-permute-done.a1), channel_id=1, source_target_pairs={{0,32},{32,0},{1,33},{33,1},{2,34},{34,2},{3,35},{35,3},{4,36},{36... | collective-permute-start | bytes 786440 | tf_op jit(solution)/shard_map/ppermute | solution.py:29
  39.6 0.7 and_select_fusion
  40.3 0.1 pad_add_fusion.place
  40.4 0.4 collective-permute-done.2.b1
  40.8 0.0 collective-permute-done.5.far_b
  40.8 0.0 copy-start
  40.8 0.9 copy-done
  41.7 2.8 %shard_map.46 = bf16[32,64,128]{2,1,0:T(8,128)(2,1)S(1)} custom-call(bf16[128,1024]{1,0:T(8,128)(2,1)S(1)} %copy-done, bf16[128,1024]{1,0:T(8,128)(2,1)S(1)} %collective-permute-done.1.b0, bf16[128,1024]{1,0:T(8,128)(2,1)S(1)} %collective-permute-done.a1, bf16[128,1024]{1,0:T(8,128)(2,1)S(1)} %collective-permute-done.2.b1, ...), custom_call_target="tpu_custom_call" | custom-call | flops 805306368 | bytes 2621440 | tf_op jit(solution)/shard_map/pallas_call | solution.py:65
  44.6 27.6 %all_to_all.10 = bf16[32,64,128]{2,1,0:T(8,128)(2,1)S(1)} all-to-all(bf16[32,64,128]{2,1,0:T(8,128)(2,1)S(1)} %shard_map.46), channel_id=1, replica_groups=mesh['z'=8,'core'=2,'y'=8,'x'=4] {'y','x'}, dimensions={0} | all-to-all | bytes 1048576 | tf_op jit(solution)/shard_map/all_to_all | solution.py:155
  72.2 0.1 convert_reduce_fusion
  72.3 0.7 collective-permute-start.6
  73.0 0.0 collective-permute-done.6
  73.0 0.1 broadcast_in_dim.10
  73.1 28.2 %all_to_all.11.slots = bf16[32,64,128]{2,1,0:T(8,128)(2,1)S(1)} all-to-all(bf16[32,64,128]{2,1,0:T(8,128)(2,1)S(1)} %broadcast_in_dim.10), channel_id=1, replica_groups=mesh['z'=8,'core'=2,'y'=8,'x'=4] {'y','x'}, dimensions={0} | all-to-all | bytes 1048576 | tf_op jit(solution)/shard_map/all_to_all | solution.py:159
  101.3 0.0 all-gather.2.cloned.1.call-done
  101.3 6.4 %shard_map.47 = f32[128,1024]{1,0:T(8,128)} custom-call(s32[9]{0:T(128)S(1)} %pad_add_fusion.place, f32[1]{0:T(128)S(6)} %mul.4.half, bf16[32,64,128]{2,1,0:T(8,128)(2,1)S(1)} %all_to_all.11.slots, bf16[32,128,1024]{2,1,0:T(8,128)(2,1)} %bitcast.4), custom_call_target="tpu_custom_call" | custom-call | flops 1073741824 | bytes 10485760 | tf_op jit(solution)/shard_map/pallas_call | solution.py:106
  (2 shorter events, 0.1 us)
Async XLA Ops:
  6.5 94.8 %all-gather.2.cloned.1.call-start = ((), (), s32[]{:S(2)}) async-start(), calls=%async_computation.2 | async-start | bytes 8912896 | tf_op jit(solution)/shard_map/all_gather | solution.py:152
  6.5 17.4 %collective-permute-start = (bf16[128,1024]{1,0:T(8,128)(2,1)}, bf16[128,1024]{1,0:T(8,128)(2,1)S(1)}, u32[]{:S(2)}, u32[]{:S(2)}) collective-permute-start(bf16[128,1024]{1,0:T(8,128)(2,1)} %source.1), channel_id=1, source_target_pairs={{0,64},{64,128},{128,192},{192,256},{256,320},{320,384},{384,448},... | collective-permute-start | bytes 786440 | tf_op jit(solution)/shard_map/ppermute | solution.py:25
  10.8 13.2 %collective-permute-start.1 = (bf16[128,1024]{1,0:T(8,128)(2,1)}, bf16[128,1024]{1,0:T(8,128)(2,1)S(1)}, u32[]{:S(2)}, u32[]{:S(2)}) collective-permute-start(bf16[128,1024]{1,0:T(8,128)(2,1)} %source.1), channel_id=1, source_target_pairs={{0,32},{32,0},{1,33},{33,1},{2,34},{34,2},{3,35},{35,3},{4,36},{36... | collective-permute-start | bytes 786440 | tf_op jit(solution)/shard_map/ppermute | solution.py:29
  12.7 21.7 %collective-permute-start.4 = (bf16[128,1024]{1,0:T(8,128)(2,1)}, bf16[128,1024]{1,0:T(8,128)(2,1)S(1)}, u32[]{:S(2)}, u32[]{:S(2)}) collective-permute-start(bf16[128,1024]{1,0:T(8,128)(2,1)} %source.1), channel_id=1, source_target_pairs={{0,384},{64,448},{128,0},{192,64},{256,128},{320,192},{384,256},{4... | collective-permute-start | bytes 786440 | tf_op jit(solution)/shard_map/ppermute | solution.py:25
  24.0 10.6 %collective-permute-start.3 = (bf16[128,1024]{1,0:T(8,128)(2,1)S(1)}, bf16[128,1024]{1,0:T(8,128)(2,1)S(1)}, u32[]{:S(2)}, u32[]{:S(2)}) collective-permute-start(bf16[128,1024]{1,0:T(8,128)(2,1)S(1)} %collective-permute-done.a1), channel_id=1, source_target_pairs={{0,64},{64,128},{128,192},{192,256},{256,320},{320,384},{384,448},... | collective-permute-start | bytes 786440 | tf_op jit(solution)/shard_map/ppermute | solution.py:25
  34.6 6.1 %collective-permute-start.5 = (bf16[256,1024]{1,0:T(8,128)(2,1)S(1)}, bf16[256,1024]{1,0:T(8,128)(2,1)S(1)}, u32[]{:S(2)}, u32[]{:S(2)}) collective-permute-start(bf16[256,1024]{1,0:T(8,128)(2,1)S(1)} %pad_maximum_fusion.1.far), channel_id=1, source_target_pairs={{0,32},{32,0},{1,33},{33,1},{2,34},{34,2},{3,35},{35,3},{4,36},{36... | collective-permute-start | bytes 1572872 | tf_op jit(solution)/shard_map/ppermute | solution.py:29
  37.2 3.6 %collective-permute-start.2 = (bf16[128,1024]{1,0:T(8,128)(2,1)S(1)}, bf16[128,1024]{1,0:T(8,128)(2,1)S(1)}, u32[]{:S(2)}, u32[]{:S(2)}) collective-permute-start(bf16[128,1024]{1,0:T(8,128)(2,1)S(1)} %collective-permute-done.a1), channel_id=1, source_target_pairs={{0,32},{32,0},{1,33},{33,1},{2,34},{34,2},{3,35},{35,3},{4,36},{36... | collective-permute-start | bytes 786440 | tf_op jit(solution)/shard_map/ppermute | solution.py:29
  40.8 1.0 copy-start
  72.3 0.7 collective-permute-start.6
Sparse Core Ops, SparseCore 0:
  34.8 59.2 all-gather.1

commit v4 on v3

v4 whole, which is shorter than its diff:
```python
import jax
import jax.numpy as jnp
import numpy as np
from jax import lax
from jax.experimental import pallas as pl
from jax.experimental.pallas import tpu as pltpu
from jax.sharding import Mesh, PartitionSpec as P

DOM = ("z", "core")
FIELD = ("y", "x")
NZ, NC, NY, NX = 8, 2, 8, 4
NF = NY * NX
ROWS, COLS = 128, 1024
VMEM = 48 * 1024 * 1024
OFFSETS = (0, -1, -2, 2, 1, 3, 4, -3)


def dot_rows(left, right):
    return lax.dot_general(
        left, right, (((1,), (1,)), ((), ())), preferred_element_type=jnp.float32
    )


def shift(array, hops):
    return lax.ppermute(array, "z", [(i, (i + hops) % NZ) for i in range(NZ)])


def other_core(array):
    return lax.ppermute(array, "core", [(0, 1), (1, 0)])


def partial_body(a1, b1, far, far_b, out, held, arrived):
    rows = [pl.ds(i * ROWS, ROWS) for i in range(3)]
    sources = (far.at[rows[0]], far_b.at[rows[0]], a1, b1)
    sources += (far.at[rows[1]], far_b.at[rows[1]], far.at[rows[2]], far_b.at[rows[2]])
    copies = [
        pltpu.make_async_copy(source, held.at[i], arrived.at[i])
        for i, source in enumerate(sources)
    ]
    for copy in copies:
        copy.start()
    for copy in copies:
        copy.wait()
    ones = jnp.ones((8, COLS), jnp.bfloat16)
    norms, lanes = {}, {}
    for i in range(8):
        wide = held[i].astype(jnp.float32)
        square = wide * wide
        if i in (0, 2, 6):
            norms[i] = jnp.sum(square, axis=1, keepdims=True)
        top = square.astype(jnp.bfloat16)
        rest = (square - top.astype(jnp.float32)).astype(jnp.bfloat16)
        lanes[i] = (dot_rows(ones, top) + dot_rows(ones, rest))[0:1]
    for row, first, columns in ((0, 0, range(8)), (2, 16, (0, 1, 6, 7)), (6, 24, (4, 5, 2, 3))):
        for j, col in enumerate(columns):
            gram = dot_rows(held[row], held[col])
            part = (norms[row] + lanes[col] - 2.0 * gram).astype(jnp.bfloat16)
            block = first + (j // 2) * 4 + j % 2
            out[block] = part[:64]
            out[block + 2] = part[64:]


def partial_distances(*blocks):
    return pl.pallas_call(
        partial_body,
        out_shape=jax.ShapeDtypeStruct((NF, 64, 128), jnp.bfloat16),
        in_specs=[pl.BlockSpec(memory_space=pl.ANY)] * 4,
        out_specs=pl.BlockSpec(memory_space=pltpu.VMEM),
        scratch_shapes=[
            pltpu.VMEM((8, ROWS, COLS), jnp.bfloat16),
            pltpu.SemaphoreType.DMA((8,)),
        ],
        compiler_params=pltpu.CompilerParams(vmem_limit_bytes=VMEM),
        cost_estimate=pl.CostEstimate(
            flops=2 * 24 * ROWS * ROWS * COLS, bytes_accessed=5 << 19, transcendentals=0
        ),
    )(*blocks)


def update_body(place, half, slots, both, out, xs, gs, arrived):
    copies = [
        [
            pltpu.make_async_copy(
                both.at[place[i] + kind], held.at[i * ROWS : (i + 1) * ROWS], arrived.at[kind, i]
            )
            for i in range(NZ * NC)
        ]
        for kind, held in enumerate((xs, gs))
    ]
    for copy in copies[0] + copies[1]:
        copy.start()
    blocks = []
    for k in range(NZ):
        blocks.append(jnp.concatenate([slots[4 * k], slots[4 * k + 2]], axis=0))
        blocks.append(jnp.concatenate([slots[4 * k + 1], slots[4 * k + 3]], axis=0))
    kernel = jnp.concatenate(blocks, axis=1)
    weight = jnp.sum(kernel.astype(jnp.float32), axis=1, keepdims=True)
    tiles = [slice(start, start + 256) for start in range(0, COLS, 256)]
    middle = NZ * NC // 2
    for copy in copies[0][:middle]:
        copy.wait()
    first, second = slice(0, middle * ROWS), slice(middle * ROWS, None)
    for at in tiles:
        spread = jnp.dot(kernel[:, first], xs[first, at], preferred_element_type=jnp.float32)
        out[:, at] = weight * xs[:ROWS, at].astype(jnp.float32) - spread
    for copy in copies[0][middle:]:
        copy.wait()
    for at in tiles:
        out[:, at] -= jnp.dot(kernel[:, second], xs[second, at], preferred_element_type=jnp.float32)
    for copy in copies[1]:
        copy.wait()
    for at in tiles:
        pulled = jnp.dot(kernel, gs[:, at], preferred_element_type=jnp.float32)
        out[:, at] = (half[0] * pulled + out[:, at]) / weight


def update(place, half, slots, both):
    return pl.pallas_call(
        update_body,
        out_shape=jax.ShapeDtypeStruct((ROWS, COLS), jnp.float32),
        in_specs=[
            pl.BlockSpec(memory_space=pltpu.SMEM),
            pl.BlockSpec(memory_space=pltpu.SMEM),
            pl.BlockSpec(memory_space=pltpu.VMEM),
            pl.BlockSpec(memory_space=pl.ANY),
        ],
        out_specs=pl.BlockSpec(memory_space=pltpu.VMEM),
        scratch_shapes=[
            pltpu.VMEM((2048, COLS), jnp.bfloat16),
            pltpu.VMEM((2048, COLS), jnp.bfloat16),
            pltpu.SemaphoreType.DMA((2, NZ * NC)),
        ],
        compiler_params=pltpu.CompilerParams(vmem_limit_bytes=VMEM),
        cost_estimate=pl.CostEstimate(
            flops=4 * ROWS * 2048 * COLS, bytes_accessed=10 << 20, transcendentals=0
        ),
    )(place, half, slots, both)


def homeward():
    pairs = []
    for z in range(NZ):
        for field in range(NF):
            hops = 0 if field < 16 else (-1 if field < 24 else 2)
            pairs.append((z * NF + field, (z + hops) % NZ * NF + field))
    return pairs


def on_device(particles, gradients, kernel_scale):
    z, core = lax.axis_index("z"), lax.axis_index("core")
    index = np.arange(NZ * NC)
    chips = (z + np.array(OFFSETS, np.int32)[index // 2] + NZ) % NZ
    place = (4 * chips + 2 * ((core + index % 2) % 2)).astype(jnp.int32)
    half = 0.5 * kernel_scale
    own = jnp.concatenate([particles, gradients], axis=0)
    a1, a3 = shift(particles, 1), shift(particles, -2)
    a2 = shift(a1, 1)
    b1 = other_core(a1)
    far = jnp.concatenate([particles, a2, a3], axis=0)
    far, b1, own, place, half, whole = lax.optimization_barrier(
        (far, b1, own, place, half, 2.0 * half)
    )
    both = lax.all_gather(own, DOM, axis=0, tiled=True)
    slots = partial_distances(a1, b1, far, other_core(far))
    terms = lax.all_to_all(slots, FIELD, 0, 0, tiled=True)
    dist = jnp.maximum(jnp.sum(terms.astype(jnp.float32), axis=0), 0.0)
    piece = jnp.exp(-dist / whole[0]).astype(jnp.bfloat16)
    piece = lax.ppermute(piece, ("z",) + FIELD, homeward())
    pieces = lax.all_to_all(
        jnp.broadcast_to(piece[None], (NF, 64, 128)), FIELD, 0, 0, tiled=True
    )
    return update(place, half, pieces, both.reshape(2 * NZ * NC, ROWS, COLS))


def solution(mesh):
    fine = Mesh(mesh.devices.reshape(NZ, NC, NY, NX), DOM + FIELD)
    placed = (P(DOM, FIELD), P(DOM, FIELD), P())
    return jax.shard_map(
        on_device, mesh=fine, in_specs=placed, out_specs=P(DOM, FIELD), check_vma=False
    )
```

time: 115 us -> 112 us (0.974)
  starting transfers between devices: 23.1 us -> 20.7 us
    ppermute x3 -> x2, starting transfers between devices: 6.25 us -> 3.84 us  [other_core(): return lax.ppermute(array, 'core', [(0, 1), (1, 0)])]
    ppermute x3 -> x2, waiting for transfers between devices: 0.4 us -> 2.25 us  [other_core(): return lax.ppermute(array, 'core', [(0, 1), (1, 0)])]
    ppermute x3, waiting for transfers between devices: 8 us -> 6.65 us  [shift(): return lax.ppermute(array, 'z', [(i, (i + hops) % NZ) for i in range(NZ)])]
  transfers between devices with their start and end apart: 8 -> 7, of which waited for: 4 -> 4; matrix products, arithmetic and copies ran while one was open for 2% -> 3% of each run, Pallas kernels for 2% -> 2%
where the time goes in v4:
time: 112 us; the launch traced here: 111 us
  blocking collectives  55.3 us (49%)
  starting transfers between devices  20.7 us (18%)
  between operations  14.2 us (13%)
  waiting for transfers between devices  8.93 us (8%)
  Pallas kernels  8.37 us (7%)
  other arithmetic  3.65 us (3%)
    all_to_all x1, blocking collectives, on_device(): lax.all_to_all(jnp.broadcast_to(piece[None], (NF, 64, 128)), FIELD, 0, 0,...  27.8 us
    all_to_all x1, blocking collectives, on_device(): terms = lax.all_to_all(slots, FIELD, 0, 0, tiled=True)  27.5 us
    ppermute x3, starting transfers between devices, shift(): return lax.ppermute(array, 'z', [(i, (i + hops) % NZ) for i in range(NZ)])  16.2 us
    ppermute x3, waiting for transfers between devices, shift(): return lax.ppermute(array, 'z', [(i, (i + hops) % NZ) for i in range(NZ)])  6.65 us
    pallas_call x1, Pallas kernels, update(): pl.pallas_call(update_body, out_shape=jax.ShapeDtypeStruct((ROWS, COLS),...  5.73 us
    ppermute x2, starting transfers between devices, other_core(): return lax.ppermute(array, 'core', [(0, 1), (1, 0)])  3.84 us
    pallas_call x1, Pallas kernels, partial_distances(): pl.pallas_call(partial_body, out_shape=jax.ShapeDtypeStruct((NF, 64, 128)...  2.64 us
    ppermute x2, waiting for transfers between devices, other_core(): return lax.ppermute(array, 'core', [(0, 1), (1, 0)])  2.25 us
  transfers between devices with their start and end apart: 7, of which 4 were waited for; matrix products, arithmetic and copies ran while one was open for 3% of the time, Pallas kernels for 2%

profile of v4, /device:TPU:8, one launch (start us, length us, event | category | flops | bytes accessed | tf_op | source)
XLA Modules:
  0.0 111.2 jit_solution(8898762645306172758)
XLA Ops:
  6.5 0.0 all-gather.2.cloned.1.call-start
  6.5 4.3 %collective-permute-start = (bf16[128,1024]{1,0:T(8,128)(2,1)}, bf16[128,1024]{1,0:T(8,128)(2,1)S(1)}, u32[]{:S(2)}, u32[]{:S(2)}) collective-permute-start(bf16[128,1024]{1,0:T(8,128)(2,1)} %param.5), channel_id=1, source_target_pairs={{0,64},{64,128},{128,192},{192,256},{256,320},{320,384},{384,448},... | collective-permute-start | bytes 786440 | tf_op jit(solution)/shard_map/ppermute | solution.py:25
  10.8 10.0 %collective-permute-start.2 = (bf16[128,1024]{1,0:T(8,128)(2,1)}, bf16[128,1024]{1,0:T(8,128)(2,1)S(1)}, u32[]{:S(2)}, u32[]{:S(2)}) collective-permute-start(bf16[128,1024]{1,0:T(8,128)(2,1)} %param.5), channel_id=1, source_target_pairs={{0,384},{64,448},{128,0},{192,64},{256,128},{320,192},{384,256},{4... | collective-permute-start | bytes 786440 | tf_op jit(solution)/shard_map/ppermute | solution.py:25
  20.9 3.1 %collective-permute-done.a1 = bf16[128,1024]{1,0:T(8,128)(2,1)S(1)} collective-permute-done((bf16[128,1024]{1,0:T(8,128)(2,1)}, bf16[128,1024]{1,0:T(8,128)(2,1)S(1)}, u32[]{:S(2)}, u32[]{:S(2)}) %collective-permute-start) | collective-permute-done | bytes 262176 | tf_op jit(solution)/shard_map/ppermute | solution.py:25
  24.0 1.9 %collective-permute-start.1 = (bf16[128,1024]{1,0:T(8,128)(2,1)S(1)}, bf16[128,1024]{1,0:T(8,128)(2,1)S(1)}, u32[]{:S(2)}, u32[]{:S(2)}) collective-permute-start(bf16[128,1024]{1,0:T(8,128)(2,1)S(1)} %collective-permute-done.a1), channel_id=1, source_target_pairs={{0,64},{64,128},{128,192},{192,256},{256,320},{320,384},{384,448},... | collective-permute-start | bytes 786440 | tf_op jit(solution)/shard_map/ppermute | solution.py:25
  25.9 1.9 %collective-permute-start.3 = (bf16[128,1024]{1,0:T(8,128)(2,1)S(1)}, bf16[128,1024]{1,0:T(8,128)(2,1)S(1)}, u32[]{:S(2)}, u32[]{:S(2)}) collective-permute-start(bf16[128,1024]{1,0:T(8,128)(2,1)S(1)} %collective-permute-done.a1), channel_id=1, source_target_pairs={{0,32},{32,0},{1,33},{33,1},{2,34},{34,2},{3,35},{35,3},{4,36},{36... | collective-permute-start | bytes 786440 | tf_op jit(solution)/shard_map/ppermute | solution.py:29
  27.8 0.7 fusion.2.place
  29.2 1.9 %pad_maximum_fusion.1 = bf16[256,1024]{1,0:T(8,128)(2,1)} fusion(bf16[128,1024]{1,0:T(8,128)(2,1)} %param.6, bf16[128,1024]{1,0:T(8,128)(2,1)} %param.5), kind=kLoop, calls=%fused_computation.2 | loop fusion | flops 1048576 | bytes 1048576 | tf_op jit(solution)/shard_map/concatenate | solution.py:155
  31.0 0.8 collective-permute-done.2
  31.8 2.7 %collective-permute-done.1 = bf16[128,1024]{1,0:T(8,128)(2,1)S(1)} collective-permute-done((bf16[128,1024]{1,0:T(8,128)(2,1)S(1)}, bf16[128,1024]{1,0:T(8,128)(2,1)S(1)}, u32[]{:S(2)}, u32[]{:S(2)}) %collective-permute-start.1) | collective-permute-done | bytes 262176 | tf_op jit(solution)/shard_map/ppermute | solution.py:25
  34.6 1.0 pad_maximum_fusion.far
  35.6 0.0 collective-permute-done.3.b1
  35.6 0.0 all-gather.2.cloned.1.call-update
  35.6 1.9 %collective-permute-start.4 = (bf16[384,1024]{1,0:T(8,128)(2,1)S(1)}, bf16[384,1024]{1,0:T(8,128)(2,1)S(1)}, u32[]{:S(2)}, u32[]{:S(2)}) collective-permute-start(bf16[384,1024]{1,0:T(8,128)(2,1)S(1)} %pad_maximum_fusion.far), channel_id=1, source_target_pairs={{0,32},{32,0},{1,33},{33,1},{2,34},{34,2},{3,35},{35,3},{4,36},{36... | collective-permute-start | bytes 2359304 | tf_op jit(solution)/shard_map/ppermute | solution.py:29
  37.5 2.3 %collective-permute-done.4.far_b = bf16[384,1024]{1,0:T(8,128)(2,1)S(1)} collective-permute-done((bf16[384,1024]{1,0:T(8,128)(2,1)S(1)}, bf16[384,1024]{1,0:T(8,128)(2,1)S(1)}, u32[]{:S(2)}, u32[]{:S(2)}) %collective-permute-start.4) | collective-permute-done | bytes 786464 | tf_op jit(solution)/shard_map/ppermute | solution.py:29
  39.8 2.6 %shard_map.55 = bf16[32,64,128]{2,1,0:T(8,128)(2,1)S(1)} custom-call(bf16[128,1024]{1,0:T(8,128)(2,1)S(1)} %collective-permute-done.a1, bf16[128,1024]{1,0:T(8,128)(2,1)S(1)} %collective-permute-done.3.b1, bf16[384,1024]{1,0:T(8,128)(2,1)S(1)} %pad_maximum_fusion.far, bf16[384,1024]{1,0:T(8,128)(2,1)S(1)} %collective-permute-done.4.far_b), custom_call_target="tpu_custom_call" | custom-call | flops 805306368 | bytes 2621440 | tf_op jit(solution)/shard_map/pallas_call | solution.py:64
  42.4 27.5 %all_to_all.10 = bf16[32,64,128]{2,1,0:T(8,128)(2,1)S(1)} all-to-all(bf16[32,64,128]{2,1,0:T(8,128)(2,1)S(1)} %shard_map.55), channel_id=1, replica_groups=mesh['z'=8,'core'=2,'y'=8,'x'=4] {'y','x'}, dimensions={0} | all-to-all | bytes 1048576 | tf_op jit(solution)/shard_map/all_to_all | solution.py:165
  69.9 0.1 convert_reduce_fusion
  70.0 0.7 collective-permute-start.5
  70.7 0.0 collective-permute-done.5
  70.7 0.1 broadcast_in_dim.2
  70.8 27.8 %all_to_all.11.slots = bf16[32,64,128]{2,1,0:T(8,128)(2,1)S(1)} all-to-all(bf16[32,64,128]{2,1,0:T(8,128)(2,1)S(1)} %broadcast_in_dim.2), channel_id=1, replica_groups=mesh['z'=8,'core'=2,'y'=8,'x'=4] {'y','x'}, dimensions={0} | all-to-all | bytes 1048576 | tf_op jit(solution)/shard_map/all_to_all | solution.py:169
  98.6 0.0 all-gather.2.cloned.1.call-done
  98.6 5.7 %shard_map.56 = f32[128,1024]{1,0:T(8,128)} custom-call(s32[16]{0:T(128)S(1)} %fusion.2.place, f32[1]{0:T(128)S(6)} %mul.12.half, bf16[32,64,128]{2,1,0:T(8,128)(2,1)S(1)} %all_to_all.11.slots, bf16[32,128,1024]{2,1,0:T(8,128)(2,1)} %bitcast.3), custom_call_target="tpu_custom_call" | custom-call | flops 1073741824 | bytes 10485760 | tf_op jit(solution)/shard_map/pallas_call | solution.py:118
  (1 shorter events, 0.0 us)
Async XLA Ops:
  6.5 92.1 %all-gather.2.cloned.1.call-start = ((), (), s32[]{:S(2)}) async-start(), calls=%async_computation.2 | async-start | bytes 8912896 | tf_op jit(solution)/shard_map/all_gather | solution.py:163
  6.5 17.4 %collective-permute-start = (bf16[128,1024]{1,0:T(8,128)(2,1)}, bf16[128,1024]{1,0:T(8,128)(2,1)S(1)}, u32[]{:S(2)}, u32[]{:S(2)}) collective-permute-start(bf16[128,1024]{1,0:T(8,128)(2,1)} %param.5), channel_id=1, source_target_pairs={{0,64},{64,128},{128,192},{192,256},{256,320},{320,384},{384,448},... | collective-permute-start | bytes 786440 | tf_op jit(solution)/shard_map/ppermute | solution.py:25
  10.8 21.0 %collective-permute-start.2 = (bf16[128,1024]{1,0:T(8,128)(2,1)}, bf16[128,1024]{1,0:T(8,128)(2,1)S(1)}, u32[]{:S(2)}, u32[]{:S(2)}) collective-permute-start(bf16[128,1024]{1,0:T(8,128)(2,1)} %param.5), channel_id=1, source_target_pairs={{0,384},{64,448},{128,0},{192,64},{256,128},{320,192},{384,256},{4... | collective-permute-start | bytes 786440 | tf_op jit(solution)/shard_map/ppermute | solution.py:25
  24.0 10.6 %collective-permute-start.1 = (bf16[128,1024]{1,0:T(8,128)(2,1)S(1)}, bf16[128,1024]{1,0:T(8,128)(2,1)S(1)}, u32[]{:S(2)}, u32[]{:S(2)}) collective-permute-start(bf16[128,1024]{1,0:T(8,128)(2,1)S(1)} %collective-permute-done.a1), channel_id=1, source_target_pairs={{0,64},{64,128},{128,192},{192,256},{256,320},{320,384},{384,448},... | collective-permute-start | bytes 786440 | tf_op jit(solution)/shard_map/ppermute | solution.py:25
  25.9 9.7 %collective-permute-start.3 = (bf16[128,1024]{1,0:T(8,128)(2,1)S(1)}, bf16[128,1024]{1,0:T(8,128)(2,1)S(1)}, u32[]{:S(2)}, u32[]{:S(2)}) collective-permute-start(bf16[128,1024]{1,0:T(8,128)(2,1)S(1)} %collective-permute-done.a1), channel_id=1, source_target_pairs={{0,32},{32,0},{1,33},{33,1},{2,34},{34,2},{3,35},{35,3},{4,36},{36... | collective-permute-start | bytes 786440 | tf_op jit(solution)/shard_map/ppermute | solution.py:29
  35.6 4.2 %collective-permute-start.4 = (bf16[384,1024]{1,0:T(8,128)(2,1)S(1)}, bf16[384,1024]{1,0:T(8,128)(2,1)S(1)}, u32[]{:S(2)}, u32[]{:S(2)}) collective-permute-start(bf16[384,1024]{1,0:T(8,128)(2,1)S(1)} %pad_maximum_fusion.far), channel_id=1, source_target_pairs={{0,32},{32,0},{1,33},{33,1},{2,34},{34,2},{3,35},{35,3},{4,36},{36... | collective-permute-start | bytes 2359304 | tf_op jit(solution)/shard_map/ppermute | solution.py:29
  70.0 0.7 collective-permute-start.5
Sparse Core Ops, SparseCore 0:
  35.7 57.4 all-gather.1

commit v5 on v4

--- a/solution.py
+++ b/solution.py
@@ -29,10 +29,9 @@
     return lax.ppermute(array, "core", [(0, 1), (1, 0)])
 
 
-def partial_body(a1, b1, far, far_b, out, held, arrived):
+def partial_body(a, b, a2, out, held, arrived):
     rows = [pl.ds(i * ROWS, ROWS) for i in range(3)]
-    sources = (far.at[rows[0]], far_b.at[rows[0]], a1, b1)
-    sources += (far.at[rows[1]], far_b.at[rows[1]], far.at[rows[2]], far_b.at[rows[2]])
+    sources = [ref.at[at] for at in rows for ref in (a, b)] + [a2]
     copies = [
         pltpu.make_async_copy(source, held.at[i], arrived.at[i])
         for i, source in enumerate(sources)
@@ -43,32 +42,37 @@
         copy.wait()
     ones = jnp.ones((8, COLS), jnp.bfloat16)
     norms, lanes = {}, {}
-    for i in range(8):
+    for i in range(7):
         wide = held[i].astype(jnp.float32)
         square = wide * wide
-        if i in (0, 2, 6):
+        if i < 6:
             norms[i] = jnp.sum(square, axis=1, keepdims=True)
-        top = square.astype(jnp.bfloat16)
-        rest = (square - top.astype(jnp.float32)).astype(jnp.bfloat16)
-        lanes[i] = (dot_rows(ones, top) + dot_rows(ones, rest))[0:1]
-    for row, first, columns in ((0, 0, range(8)), (2, 16, (0, 1, 6, 7)), (6, 24, (4, 5, 2, 3))):
-        for j, col in enumerate(columns):
-            gram = dot_rows(held[row], held[col])
-            part = (norms[row] + lanes[col] - 2.0 * gram).astype(jnp.bfloat16)
-            block = first + (j // 2) * 4 + j % 2
-            out[block] = part[:64]
-            out[block + 2] = part[64:]
+        if i % 2 == 0:
+            top = square.astype(jnp.bfloat16)
+            rest = (square - top.astype(jnp.float32)).astype(jnp.bfloat16)
+            lanes[i] = (dot_rows(ones, top) + dot_rows(ones, rest))[0:1]
+    for first, pairs in (
+        (0, ((0, 0), (1, 2), (2, 6), (3, 4))),
+        (2, ((4, 0), (5, 4))),
+        (4, ((6, 6), (7, 2))),
+    ):
+        for r in range(NC):
+            for k, col in pairs:
+                gram = dot_rows(held[first + r], held[col])
+                part = (norms[first + r] + lanes[col] - 2.0 * gram).astype(jnp.bfloat16)
+                out[4 * k + r] = part[:64]
+                out[4 * k + 2 + r] = part[64:]
 
 
 def partial_distances(*blocks):
     return pl.pallas_call(
         partial_body,
         out_shape=jax.ShapeDtypeStruct((NF, 64, 128), jnp.bfloat16),
-        in_specs=[pl.BlockSpec(memory_space=pl.ANY)] * 4,
+        in_specs=[pl.BlockSpec(memory_space=pl.ANY)] * 3,
         out_specs=pl.BlockSpec(memory_space=pltpu.VMEM),
         scratch_shapes=[
-            pltpu.VMEM((8, ROWS, COLS), jnp.bfloat16),
-            pltpu.SemaphoreType.DMA((8,)),
+            pltpu.VMEM((7, ROWS, COLS), jnp.bfloat16),
+            pltpu.SemaphoreType.DMA((7,)),
         ],
         compiler_params=pltpu.CompilerParams(vmem_limit_bytes=VMEM),
         cost_estimate=pl.CostEstimate(
@@ -140,9 +144,11 @@
 def homeward():
     pairs = []
     for z in range(NZ):
-        for field in range(NF):
-            hops = 0 if field < 16 else (-1 if field < 24 else 2)
-            pairs.append((z * NF + field, (z + hops) % NZ * NF + field))
+        for core in range(NC):
+            for field in range(NF):
+                chip = (z + (0, 0, 0, 0, -1, -1, 2, 2)[field // 4]) % NZ
+                home = chip * NC + (core + field % 2) % NC
+                pairs.append(((z * NC + core) * NF + field, home * NF + field))
     return pairs
 
 
@@ -155,17 +161,16 @@
     own = jnp.concatenate([particles, gradients], axis=0)
     a1, a3 = shift(particles, 1), shift(particles, -2)
     a2 = shift(a1, 1)
-    b1 = other_core(a1)
-    far = jnp.concatenate([particles, a2, a3], axis=0)
-    far, b1, own, place, half, whole = lax.optimization_barrier(
-        (far, b1, own, place, half, 2.0 * half)
+    near = jnp.concatenate([particles, a1, a3], axis=0)
+    near, a2, own, place, half, whole = lax.optimization_barrier(
+        (near, a2, own, place, half, 2.0 * half)
     )
     both = lax.all_gather(own, DOM, axis=0, tiled=True)
-    slots = partial_distances(a1, b1, far, other_core(far))
+    slots = partial_distances(near, other_core(near), a2)
     terms = lax.all_to_all(slots, FIELD, 0, 0, tiled=True)
     dist = jnp.maximum(jnp.sum(terms.astype(jnp.float32), axis=0), 0.0)
     piece = jnp.exp(-dist / whole[0]).astype(jnp.bfloat16)
-    piece = lax.ppermute(piece, ("z",) + FIELD, homeward())
+    piece = lax.ppermute(piece, DOM + FIELD, homeward())
     pieces = lax.all_to_all(
         jnp.broadcast_to(piece[None], (NF, 64, 128)), FIELD, 0, 0, tiled=True
     )

time: 112 us -> 111 us (level)
  starting transfers between devices: 20.7 us -> 18.8 us
    ppermute x2 -> x1, starting transfers between devices: 3.84 us -> 1.92 us  [other_core(): return lax.ppermute(array, 'core', [(0, 1), (1, 0)])]
    ppermute x2 -> x1, waiting for transfers between devices: 2.25 us -> 2.25 us  [other_core(): return lax.ppermute(array, 'core', [(0, 1), (1, 0)])]
  transfers between devices with their start and end apart: 7 -> 6, of which waited for: 4 -> 4; matrix products, arithmetic and copies ran while one was open for 3% -> 3% of each run, Pallas kernels for 2% -> 2%
where the time goes in v5:
time: 111 us; the launch traced here: 110 us
  blocking collectives  56 us (50%)
  starting transfers between devices  18.8 us (17%)
  between operations  14.1 us (13%)
  waiting for transfers between devices  9.85 us (9%)
  Pallas kernels  7.87 us (7%)
  other arithmetic  3.65 us (3%)
    all_to_all x1, blocking collectives, on_device(): lax.all_to_all(jnp.broadcast_to(piece[None], (NF, 64, 128)), FIELD, 0, 0,...  28.6 us
    all_to_all x1, blocking collectives, on_device(): terms = lax.all_to_all(slots, FIELD, 0, 0, tiled=True)  27.5 us
    ppermute x3, starting transfers between devices, shift(): return lax.ppermute(array, 'z', [(i, (i + hops) % NZ) for i in range(NZ)])  16.2 us
    ppermute x3, waiting for transfers between devices, shift(): return lax.ppermute(array, 'z', [(i, (i + hops) % NZ) for i in range(NZ)])  7.58 us
    pallas_call x1, Pallas kernels, update(): pl.pallas_call(update_body, out_shape=jax.ShapeDtypeStruct((ROWS, COLS),...  5.73 us
    ppermute x1, waiting for transfers between devices, other_core(): return lax.ppermute(array, 'core', [(0, 1), (1, 0)])  2.25 us
  transfers between devices with their start and end apart: 6, of which 4 were waited for; matrix products, arithmetic and copies ran while one was open for 3% of the time, Pallas kernels for 2%

profile of v5, /device:TPU:8, one launch (start us, length us, event | category | flops | bytes accessed | tf_op | source)
XLA Modules:
  0.0 110.5 jit_solution(11055865931445798713)
XLA Ops:
  6.5 0.0 all-gather.2.cloned.1.call-start
  6.5 4.3 %collective-permute-start = (bf16[128,1024]{1,0:T(8,128)(2,1)}, bf16[128,1024]{1,0:T(8,128)(2,1)S(1)}, u32[]{:S(2)}, u32[]{:S(2)}) collective-permute-start(bf16[128,1024]{1,0:T(8,128)(2,1)} %param.5), channel_id=1, source_target_pairs={{0,64},{64,128},{128,192},{192,256},{256,320},{320,384},{384,448},... | collective-permute-start | bytes 786440 | tf_op jit(solution)/shard_map/ppermute | solution.py:25
  10.8 10.0 %collective-permute-start.1 = (bf16[128,1024]{1,0:T(8,128)(2,1)}, bf16[128,1024]{1,0:T(8,128)(2,1)S(1)}, u32[]{:S(2)}, u32[]{:S(2)}) collective-permute-start(bf16[128,1024]{1,0:T(8,128)(2,1)} %param.5), channel_id=1, source_target_pairs={{0,384},{64,448},{128,0},{192,64},{256,128},{320,192},{384,256},{4... | collective-permute-start | bytes 786440 | tf_op jit(solution)/shard_map/ppermute | solution.py:25
  20.9 3.1 %collective-permute-done = bf16[128,1024]{1,0:T(8,128)(2,1)S(1)} collective-permute-done((bf16[128,1024]{1,0:T(8,128)(2,1)}, bf16[128,1024]{1,0:T(8,128)(2,1)S(1)}, u32[]{:S(2)}, u32[]{:S(2)}) %collective-permute-start) | collective-permute-done | bytes 262176 | tf_op jit(solution)/shard_map/ppermute | solution.py:25
  24.0 1.9 %collective-permute-start.2 = (bf16[128,1024]{1,0:T(8,128)(2,1)S(1)}, bf16[128,1024]{1,0:T(8,128)(2,1)S(1)}, u32[]{:S(2)}, u32[]{:S(2)}) collective-permute-start(bf16[128,1024]{1,0:T(8,128)(2,1)S(1)} %collective-permute-done), channel_id=1, source_target_pairs={{0,64},{64,128},{128,192},{192,256},{256,320},{320,384},{384,448},... | collective-permute-start | bytes 786440 | tf_op jit(solution)/shard_map/ppermute | solution.py:25
  25.9 0.7 fusion.2.place
  27.2 1.9 %pad_maximum_fusion.1 = bf16[256,1024]{1,0:T(8,128)(2,1)} fusion(bf16[128,1024]{1,0:T(8,128)(2,1)} %param.6, bf16[128,1024]{1,0:T(8,128)(2,1)} %param.5), kind=kLoop, calls=%fused_computation.2 | loop fusion | flops 1048576 | bytes 1048576 | tf_op jit(solution)/shard_map/concatenate | solution.py:161
  29.1 2.7 %collective-permute-done.1 = bf16[128,1024]{1,0:T(8,128)(2,1)S(1)} collective-permute-done((bf16[128,1024]{1,0:T(8,128)(2,1)}, bf16[128,1024]{1,0:T(8,128)(2,1)S(1)}, u32[]{:S(2)}, u32[]{:S(2)}) %collective-permute-start.1) | collective-permute-done | bytes 262176 | tf_op jit(solution)/shard_map/ppermute | solution.py:25
  31.8 1.0 pad_maximum_fusion.a
  32.8 1.7 %collective-permute-done.2.a2 = bf16[128,1024]{1,0:T(8,128)(2,1)S(1)} collective-permute-done((bf16[128,1024]{1,0:T(8,128)(2,1)S(1)}, bf16[128,1024]{1,0:T(8,128)(2,1)S(1)}, u32[]{:S(2)}, u32[]{:S(2)}) %collective-permute-start.2) | collective-permute-done | bytes 262176 | tf_op jit(solution)/shard_map/ppermute | solution.py:25
  34.6 0.0 all-gather.2.cloned.1.call-update
  34.6 1.9 %collective-permute-start.3 = (bf16[384,1024]{1,0:T(8,128)(2,1)S(1)}, bf16[384,1024]{1,0:T(8,128)(2,1)S(1)}, u32[]{:S(2)}, u32[]{:S(2)}) collective-permute-start(bf16[384,1024]{1,0:T(8,128)(2,1)S(1)} %pad_maximum_fusion.a), channel_id=1, source_target_pairs={{0,32},{32,0},{1,33},{33,1},{2,34},{34,2},{3,35},{35,3},{4,36},{36... | collective-permute-start | bytes 2359304 | tf_op jit(solution)/shard_map/ppermute | solution.py:29
  36.5 2.3 %collective-permute-done.3.b = bf16[384,1024]{1,0:T(8,128)(2,1)S(1)} collective-permute-done((bf16[384,1024]{1,0:T(8,128)(2,1)S(1)}, bf16[384,1024]{1,0:T(8,128)(2,1)S(1)}, u32[]{:S(2)}, u32[]{:S(2)}) %collective-permute-start.3) | collective-permute-done | bytes 786464 | tf_op jit(solution)/shard_map/ppermute | solution.py:29
  38.8 2.1 %shard_map.55 = bf16[32,64,128]{2,1,0:T(8,128)(2,1)S(1)} custom-call(bf16[384,1024]{1,0:T(8,128)(2,1)S(1)} %pad_maximum_fusion.a, bf16[384,1024]{1,0:T(8,128)(2,1)S(1)} %collective-permute-done.3.b, bf16[128,1024]{1,0:T(8,128)(2,1)S(1)} %collective-permute-done.2.a2), custom_call_target="tpu_custom_call" | custom-call | flops 805306368 | bytes 2621440 | tf_op jit(solution)/shard_map/pallas_call | solution.py:68
  40.9 27.5 %all_to_all.10 = bf16[32,64,128]{2,1,0:T(8,128)(2,1)S(1)} all-to-all(bf16[32,64,128]{2,1,0:T(8,128)(2,1)S(1)} %shard_map.55), channel_id=1, replica_groups=mesh['z'=8,'core'=2,'y'=8,'x'=4] {'y','x'}, dimensions={0} | all-to-all | bytes 1048576 | tf_op jit(solution)/shard_map/all_to_all | solution.py:170
  68.4 0.1 convert_reduce_fusion
  68.5 0.7 collective-permute-start.4
  69.2 0.0 collective-permute-done.4
  69.2 0.1 broadcast_in_dim.2
  69.3 28.6 %all_to_all.11.slots = bf16[32,64,128]{2,1,0:T(8,128)(2,1)S(1)} all-to-all(bf16[32,64,128]{2,1,0:T(8,128)(2,1)S(1)} %broadcast_in_dim.2), channel_id=1, replica_groups=mesh['z'=8,'core'=2,'y'=8,'x'=4] {'y','x'}, dimensions={0} | all-to-all | bytes 1048576 | tf_op jit(solution)/shard_map/all_to_all | solution.py:174
  97.9 0.0 all-gather.2.cloned.1.call-done
  97.9 5.7 %shard_map.56 = f32[128,1024]{1,0:T(8,128)} custom-call(s32[16]{0:T(128)S(1)} %fusion.2.place, f32[1]{0:T(128)S(6)} %mul.12.half, bf16[32,64,128]{2,1,0:T(8,128)(2,1)S(1)} %all_to_all.11.slots, bf16[32,128,1024]{2,1,0:T(8,128)(2,1)} %bitcast.3), custom_call_target="tpu_custom_call" | custom-call | flops 1073741824 | bytes 10485760 | tf_op jit(solution)/shard_map/pallas_call | solution.py:122
  (1 shorter events, 0.0 us)
Async XLA Ops:
  6.5 91.3 %all-gather.2.cloned.1.call-start = ((), (), s32[]{:S(2)}) async-start(), calls=%async_computation.2 | async-start | bytes 8912896 | tf_op jit(solution)/shard_map/all_gather | solution.py:168
  6.5 17.4 %collective-permute-start = (bf16[128,1024]{1,0:T(8,128)(2,1)}, bf16[128,1024]{1,0:T(8,128)(2,1)S(1)}, u32[]{:S(2)}, u32[]{:S(2)}) collective-permute-start(bf16[128,1024]{1,0:T(8,128)(2,1)} %param.5), channel_id=1, source_target_pairs={{0,64},{64,128},{128,192},{192,256},{256,320},{320,384},{384,448},... | collective-permute-start | bytes 786440 | tf_op jit(solution)/shard_map/ppermute | solution.py:25
  10.8 21.0 %collective-permute-start.1 = (bf16[128,1024]{1,0:T(8,128)(2,1)}, bf16[128,1024]{1,0:T(8,128)(2,1)S(1)}, u32[]{:S(2)}, u32[]{:S(2)}) collective-permute-start(bf16[128,1024]{1,0:T(8,128)(2,1)} %param.5), channel_id=1, source_target_pairs={{0,384},{64,448},{128,0},{192,64},{256,128},{320,192},{384,256},{4... | collective-permute-start | bytes 786440 | tf_op jit(solution)/shard_map/ppermute | solution.py:25
  24.0 10.6 %collective-permute-start.2 = (bf16[128,1024]{1,0:T(8,128)(2,1)S(1)}, bf16[128,1024]{1,0:T(8,128)(2,1)S(1)}, u32[]{:S(2)}, u32[]{:S(2)}) collective-permute-start(bf16[128,1024]{1,0:T(8,128)(2,1)S(1)} %collective-permute-done), channel_id=1, source_target_pairs={{0,64},{64,128},{128,192},{192,256},{256,320},{320,384},{384,448},... | collective-permute-start | bytes 786440 | tf_op jit(solution)/shard_map/ppermute | solution.py:25
  34.6 4.2 %collective-permute-start.3 = (bf16[384,1024]{1,0:T(8,128)(2,1)S(1)}, bf16[384,1024]{1,0:T(8,128)(2,1)S(1)}, u32[]{:S(2)}, u32[]{:S(2)}) collective-permute-start(bf16[384,1024]{1,0:T(8,128)(2,1)S(1)} %pad_maximum_fusion.a), channel_id=1, source_target_pairs={{0,32},{32,0},{1,33},{33,1},{2,34},{34,2},{3,35},{35,3},{4,36},{36... | collective-permute-start | bytes 2359304 | tf_op jit(solution)/shard_map/ppermute | solution.py:29
  68.5 0.7 collective-permute-start.4
Sparse Core Ops, SparseCore 0:
  34.7 57.6 all-gather.1

commit v6 on v5

--- a/solution.py
+++ b/solution.py
@@ -81,13 +81,15 @@
     )(*blocks)
 
 
-def update_body(place, half, slots, both, out, xs, gs, arrived):
+def update_body(place, half, slots, near, near_b, a2, both, out, xs, gs, arrived):
+    here = {0: (near, 0), 1: (near_b, 0), 2: (near, 1), 3: (near_b, 1), 4: (a2, 0), 6: (near, 2), 7: (near_b, 2)}
     copies = [
         [
             pltpu.make_async_copy(
                 both.at[place[i] + kind], held.at[i * ROWS : (i + 1) * ROWS], arrived.at[kind, i]
             )
             for i in range(NZ * NC)
+            if kind == 1 or i not in here
         ]
         for kind, held in enumerate((xs, gs))
     ]
@@ -100,17 +102,19 @@
     kernel = jnp.concatenate(blocks, axis=1)
     weight = jnp.sum(kernel.astype(jnp.float32), axis=1, keepdims=True)
     tiles = [slice(start, start + 256) for start in range(0, COLS, 256)]
-    middle = NZ * NC // 2
-    for copy in copies[0][:middle]:
+    for copy in copies[0]:
         copy.wait()
-    first, second = slice(0, middle * ROWS), slice(middle * ROWS, None)
+
+    def coords(at):
+        parts = []
+        for i in range(NZ * NC):
+            ref, j = here.get(i, (xs, i))
+            parts.append(ref[j * ROWS : (j + 1) * ROWS, at])
+        return jnp.concatenate(parts, axis=0)
+
     for at in tiles:
-        spread = jnp.dot(kernel[:, first], xs[first, at], preferred_element_type=jnp.float32)
-        out[:, at] = weight * xs[:ROWS, at].astype(jnp.float32) - spread
-    for copy in copies[0][middle:]:
-        copy.wait()
-    for at in tiles:
-        out[:, at] -= jnp.dot(kernel[:, second], xs[second, at], preferred_element_type=jnp.float32)
+        spread = jnp.dot(kernel, coords(at), preferred_element_type=jnp.float32)
+        out[:, at] = weight * near[:ROWS, at].astype(jnp.float32) - spread
     for copy in copies[1]:
         copy.wait()
     for at in tiles:
@@ -118,13 +122,16 @@
         out[:, at] = (half[0] * pulled + out[:, at]) / weight
 
 
-def update(place, half, slots, both):
+def update(place, half, slots, near, near_b, a2, both):
     return pl.pallas_call(
         update_body,
         out_shape=jax.ShapeDtypeStruct((ROWS, COLS), jnp.float32),
         in_specs=[
             pl.BlockSpec(memory_space=pltpu.SMEM),
             pl.BlockSpec(memory_space=pltpu.SMEM),
+            pl.BlockSpec(memory_space=pltpu.VMEM),
+            pl.BlockSpec(memory_space=pltpu.VMEM),
+            pl.BlockSpec(memory_space=pltpu.VMEM),
             pl.BlockSpec(memory_space=pltpu.VMEM),
             pl.BlockSpec(memory_space=pl.ANY),
         ],
@@ -138,7 +145,7 @@
         cost_estimate=pl.CostEstimate(
             flops=4 * ROWS * 2048 * COLS, bytes_accessed=10 << 20, transcendentals=0
         ),
-    )(place, half, slots, both)
+    )(place, half, slots, near, near_b, a2, both)
 
 
 def homeward():
@@ -166,7 +173,8 @@
         (near, a2, own, place, half, 2.0 * half)
     )
     both = lax.all_gather(own, DOM, axis=0, tiled=True)
-    slots = partial_distances(near, other_core(near), a2)
+    near_b = other_core(near)
+    slots = partial_distances(near, near_b, a2)
     terms = lax.all_to_all(slots, FIELD, 0, 0, tiled=True)
     dist = jnp.maximum(jnp.sum(terms.astype(jnp.float32), axis=0), 0.0)
     piece = jnp.exp(-dist / whole[0]).astype(jnp.bfloat16)
@@ -174,7 +182,7 @@
     pieces = lax.all_to_all(
         jnp.broadcast_to(piece[None], (NF, 64, 128)), FIELD, 0, 0, tiled=True
     )
-    return update(place, half, pieces, both.reshape(2 * NZ * NC, ROWS, COLS))
+    return update(place, half, pieces, near, near_b, a2, both.reshape(2 * NZ * NC, ROWS, COLS))
 
 
 def solution(mesh):

time: 111 us -> 110 us (level)
  no operation moved by 1% of the time
where the time goes in v6:
time: 110 us
  blocking collectives  56 us (51%)
  starting transfers between devices  18.8 us (17%)
  between operations  14.1 us (13%)
  waiting for transfers between devices  9.85 us (9%)
  Pallas kernels  7.34 us (7%)
  other arithmetic  3.65 us (3%)
    all_to_all x1, blocking collectives, on_device(): lax.all_to_all(jnp.broadcast_to(piece[None], (NF, 64, 128)), FIELD, 0, 0,...  28.6 us
    all_to_all x1, blocking collectives, on_device(): terms = lax.all_to_all(slots, FIELD, 0, 0, tiled=True)  27.5 us
    ppermute x3, starting transfers between devices, shift(): return lax.ppermute(array, 'z', [(i, (i + hops) % NZ) for i in range(NZ)])  16.2 us
    ppermute x3, waiting for transfers between devices, shift(): return lax.ppermute(array, 'z', [(i, (i + hops) % NZ) for i in range(NZ)])  7.58 us
    pallas_call x1, Pallas kernels, update(): pl.pallas_call(update_body, out_shape=jax.ShapeDtypeStruct((ROWS, COLS),...  5.2 us
    ppermute x1, waiting for transfers between devices, other_core(): return lax.ppermute(array, 'core', [(0, 1), (1, 0)])  2.25 us
  transfers between devices with their start and end apart: 6, of which 4 were waited for; matrix products, arithmetic and copies ran while one was open for 3% of the time, Pallas kernels for 2%

profile of v6, /device:TPU:8, one launch (start us, length us, event | category | flops | bytes accessed | tf_op | source)
XLA Modules:
  0.0 109.9 jit_solution(13758866607953129313)
XLA Ops:
  6.5 0.0 all-gather.2.cloned.1.call-start
  6.5 4.3 %collective-permute-start = (bf16[128,1024]{1,0:T(8,128)(2,1)}, bf16[128,1024]{1,0:T(8,128)(2,1)S(1)}, u32[]{:S(2)}, u32[]{:S(2)}) collective-permute-start(bf16[128,1024]{1,0:T(8,128)(2,1)} %param.5), channel_id=1, source_target_pairs={{0,64},{64,128},{128,192},{192,256},{256,320},{320,384},{384,448},... | collective-permute-start | bytes 786440 | tf_op jit(solution)/shard_map/ppermute | solution.py:25
  10.8 10.0 %collective-permute-start.1 = (bf16[128,1024]{1,0:T(8,128)(2,1)}, bf16[128,1024]{1,0:T(8,128)(2,1)S(1)}, u32[]{:S(2)}, u32[]{:S(2)}) collective-permute-start(bf16[128,1024]{1,0:T(8,128)(2,1)} %param.5), channel_id=1, source_target_pairs={{0,384},{64,448},{128,0},{192,64},{256,128},{320,192},{384,256},{4... | collective-permute-start | bytes 786440 | tf_op jit(solution)/shard_map/ppermute | solution.py:25
  20.9 3.1 %collective-permute-done = bf16[128,1024]{1,0:T(8,128)(2,1)S(1)} collective-permute-done((bf16[128,1024]{1,0:T(8,128)(2,1)}, bf16[128,1024]{1,0:T(8,128)(2,1)S(1)}, u32[]{:S(2)}, u32[]{:S(2)}) %collective-permute-start) | collective-permute-done | bytes 262176 | tf_op jit(solution)/shard_map/ppermute | solution.py:25
  24.0 1.9 %collective-permute-start.2 = (bf16[128,1024]{1,0:T(8,128)(2,1)S(1)}, bf16[128,1024]{1,0:T(8,128)(2,1)S(1)}, u32[]{:S(2)}, u32[]{:S(2)}) collective-permute-start(bf16[128,1024]{1,0:T(8,128)(2,1)S(1)} %collective-permute-done), channel_id=1, source_target_pairs={{0,64},{64,128},{128,192},{192,256},{256,320},{320,384},{384,448},... | collective-permute-start | bytes 786440 | tf_op jit(solution)/shard_map/ppermute | solution.py:25
  25.9 0.7 fusion.2.place
  27.2 1.9 %pad_maximum_fusion.1 = bf16[256,1024]{1,0:T(8,128)(2,1)} fusion(bf16[128,1024]{1,0:T(8,128)(2,1)} %param.6, bf16[128,1024]{1,0:T(8,128)(2,1)} %param.5), kind=kLoop, calls=%fused_computation.2 | loop fusion | flops 1048576 | bytes 1048576 | tf_op jit(solution)/shard_map/concatenate | solution.py:168
  29.1 2.7 %collective-permute-done.1 = bf16[128,1024]{1,0:T(8,128)(2,1)S(1)} collective-permute-done((bf16[128,1024]{1,0:T(8,128)(2,1)}, bf16[128,1024]{1,0:T(8,128)(2,1)S(1)}, u32[]{:S(2)}, u32[]{:S(2)}) %collective-permute-start.1) | collective-permute-done | bytes 262176 | tf_op jit(solution)/shard_map/ppermute | solution.py:25
  31.8 1.0 pad_maximum_fusion.a.near
  32.8 1.7 %collective-permute-done.2.a2 = bf16[128,1024]{1,0:T(8,128)(2,1)S(1)} collective-permute-done((bf16[128,1024]{1,0:T(8,128)(2,1)S(1)}, bf16[128,1024]{1,0:T(8,128)(2,1)S(1)}, u32[]{:S(2)}, u32[]{:S(2)}) %collective-permute-start.2) | collective-permute-done | bytes 262176 | tf_op jit(solution)/shard_map/ppermute | solution.py:25
  34.6 0.0 all-gather.2.cloned.1.call-update
  34.6 1.9 %collective-permute-start.3 = (bf16[384,1024]{1,0:T(8,128)(2,1)S(1)}, bf16[384,1024]{1,0:T(8,128)(2,1)S(1)}, u32[]{:S(2)}, u32[]{:S(2)}) collective-permute-start(bf16[384,1024]{1,0:T(8,128)(2,1)S(1)} %pad_maximum_fusion.a.near), channel_id=1, source_target_pairs={{0,32},{32,0},{1,33},{33,1},{2,34},{34,2},{3,35},{35,3},{4,36},{36... | collective-permute-start | bytes 2359304 | tf_op jit(solution)/shard_map/ppermute | solution.py:29
  36.5 2.3 %collective-permute-done.3.b.near_b = bf16[384,1024]{1,0:T(8,128)(2,1)S(1)} collective-permute-done((bf16[384,1024]{1,0:T(8,128)(2,1)S(1)}, bf16[384,1024]{1,0:T(8,128)(2,1)S(1)}, u32[]{:S(2)}, u32[]{:S(2)}) %collective-permute-start.3) | collective-permute-done | bytes 786464 | tf_op jit(solution)/shard_map/ppermute | solution.py:29
  38.8 2.1 %shard_map.55 = bf16[32,64,128]{2,1,0:T(8,128)(2,1)S(1)} custom-call(bf16[384,1024]{1,0:T(8,128)(2,1)S(1)} %pad_maximum_fusion.a.near, bf16[384,1024]{1,0:T(8,128)(2,1)S(1)} %collective-permute-done.3.b.near_b, bf16[128,1024]{1,0:T(8,128)(2,1)S(1)} %collective-permute-done.2.a2), custom_call_target="tpu_custom_call" | custom-call | flops 805306368 | bytes 2621440 | tf_op jit(solution)/shard_map/pallas_call | solution.py:68
  40.9 27.5 %all_to_all.10 = bf16[32,64,128]{2,1,0:T(8,128)(2,1)S(1)} all-to-all(bf16[32,64,128]{2,1,0:T(8,128)(2,1)S(1)} %shard_map.55), channel_id=1, replica_groups=mesh['z'=8,'core'=2,'y'=8,'x'=4] {'y','x'}, dimensions={0} | all-to-all | bytes 1048576 | tf_op jit(solution)/shard_map/all_to_all | solution.py:178
  68.4 0.1 convert_reduce_fusion
  68.5 0.7 collective-permute-start.4
  69.2 0.0 collective-permute-done.4
  69.2 0.1 broadcast_in_dim.2
  69.3 28.6 %all_to_all.11.slots = bf16[32,64,128]{2,1,0:T(8,128)(2,1)S(1)} all-to-all(bf16[32,64,128]{2,1,0:T(8,128)(2,1)S(1)} %broadcast_in_dim.2), channel_id=1, replica_groups=mesh['z'=8,'core'=2,'y'=8,'x'=4] {'y','x'}, dimensions={0} | all-to-all | bytes 1048576 | tf_op jit(solution)/shard_map/all_to_all | solution.py:182
  97.9 0.0 all-gather.2.cloned.1.call-done
  97.9 5.2 %shard_map.56 = f32[128,1024]{1,0:T(8,128)} custom-call(s32[16]{0:T(128)S(1)} %fusion.2.place, f32[1]{0:T(128)S(6)} %mul.12.half, bf16[32,64,128]{2,1,0:T(8,128)(2,1)S(1)} %all_to_all.11.slots, bf16[384,1024]{1,0:T(8,128)(2,1)S(1)} %pad_maximum_fusion.a.near, bf16[384,1024]{1,0:T(8,128)(2,1)S(1)} %collective-permute-done.3.b.near_b, ...), custom_call_target="tpu_custom_call" | custom-call | flops 1073741824 | bytes 10485760 | tf_op jit(solution)/shard_map/pallas_call | solution.py:126
  (1 shorter events, 0.0 us)
Async XLA Ops:
  6.5 91.3 %all-gather.2.cloned.1.call-start = ((), (), s32[]{:S(2)}) async-start(), calls=%async_computation.2 | async-start | bytes 8912896 | tf_op jit(solution)/shard_map/all_gather | solution.py:175
  6.5 17.4 %collective-permute-start = (bf16[128,1024]{1,0:T(8,128)(2,1)}, bf16[128,1024]{1,0:T(8,128)(2,1)S(1)}, u32[]{:S(2)}, u32[]{:S(2)}) collective-permute-start(bf16[128,1024]{1,0:T(8,128)(2,1)} %param.5), channel_id=1, source_target_pairs={{0,64},{64,128},{128,192},{192,256},{256,320},{320,384},{384,448},... | collective-permute-start | bytes 786440 | tf_op jit(solution)/shard_map/ppermute | solution.py:25
  10.8 21.0 %collective-permute-start.1 = (bf16[128,1024]{1,0:T(8,128)(2,1)}, bf16[128,1024]{1,0:T(8,128)(2,1)S(1)}, u32[]{:S(2)}, u32[]{:S(2)}) collective-permute-start(bf16[128,1024]{1,0:T(8,128)(2,1)} %param.5), channel_id=1, source_target_pairs={{0,384},{64,448},{128,0},{192,64},{256,128},{320,192},{384,256},{4... | collective-permute-start | bytes 786440 | tf_op jit(solution)/shard_map/ppermute | solution.py:25
  24.0 10.6 %collective-permute-start.2 = (bf16[128,1024]{1,0:T(8,128)(2,1)S(1)}, bf16[128,1024]{1,0:T(8,128)(2,1)S(1)}, u32[]{:S(2)}, u32[]{:S(2)}) collective-permute-start(bf16[128,1024]{1,0:T(8,128)(2,1)S(1)} %collective-permute-done), channel_id=1, source_target_pairs={{0,64},{64,128},{128,192},{192,256},{256,320},{320,384},{384,448},... | collective-permute-start | bytes 786440 | tf_op jit(solution)/shard_map/ppermute | solution.py:25
  34.6 4.2 %collective-permute-start.3 = (bf16[384,1024]{1,0:T(8,128)(2,1)S(1)}, bf16[384,1024]{1,0:T(8,128)(2,1)S(1)}, u32[]{:S(2)}, u32[]{:S(2)}) collective-permute-start(bf16[384,1024]{1,0:T(8,128)(2,1)S(1)} %pad_maximum_fusion.a.near), channel_id=1, source_target_pairs={{0,32},{32,0},{1,33},{33,1},{2,34},{34,2},{3,35},{35,3},{4,36},{36... | collective-permute-start | bytes 2359304 | tf_op jit(solution)/shard_map/ppermute | solution.py:29
  68.5 0.7 collective-permute-start.4
Sparse Core Ops, SparseCore 0:
  34.7 57.6 all-gather.1

commit v7 on v6

--- a/solution.py
+++ b/solution.py
@@ -169,11 +169,11 @@
     a1, a3 = shift(particles, 1), shift(particles, -2)
     a2 = shift(a1, 1)
     near = jnp.concatenate([particles, a1, a3], axis=0)
-    near, a2, own, place, half, whole = lax.optimization_barrier(
+    near_b = other_core(near)
+    _, a2, own, place, half, whole = lax.optimization_barrier(
         (near, a2, own, place, half, 2.0 * half)
     )
     both = lax.all_gather(own, DOM, axis=0, tiled=True)
-    near_b = other_core(near)
     slots = partial_distances(near, near_b, a2)
     terms = lax.all_to_all(slots, FIELD, 0, 0, tiled=True)
     dist = jnp.maximum(jnp.sum(terms.astype(jnp.float32), axis=0), 0.0)

time: 110 us -> 110 us (level)
  no operation moved by 1% of the time
where the time goes in v7:
time: 110 us
  blocking collectives  56 us (51%)
  starting transfers between devices  18.8 us (17%)
  between operations  14.2 us (13%)
  waiting for transfers between devices  9.83 us (9%)
  Pallas kernels  7.34 us (7%)
  other arithmetic  2.65 us (2%)
  local copies, waits for them, and re-layouts  1.12 us (1%)
    all_to_all x1, blocking collectives, on_device(): lax.all_to_all(jnp.broadcast_to(piece[None], (NF, 64, 128)), FIELD, 0, 0,...  28.6 us
    all_to_all x1, blocking collectives, on_device(): terms = lax.all_to_all(slots, FIELD, 0, 0, tiled=True)  27.5 us
    ppermute x3, starting transfers between devices, shift(): return lax.ppermute(array, 'z', [(i, (i + hops) % NZ) for i in range(NZ)])  16.2 us
    ppermute x3, waiting for transfers between devices, shift(): return lax.ppermute(array, 'z', [(i, (i + hops) % NZ) for i in range(NZ)])  7.56 us
    pallas_call x1, Pallas kernels, update(): pl.pallas_call(update_body, out_shape=jax.ShapeDtypeStruct((ROWS, COLS),...  5.2 us
    ppermute x1, waiting for transfers between devices, other_core(): return lax.ppermute(array, 'core', [(0, 1), (1, 0)])  2.25 us
  transfers between devices with their start and end apart: 6, of which 4 were waited for; matrix products, arithmetic and copies ran while one was open for 3% of the time, Pallas kernels for 2%

profile of v7, /device:TPU:8, one launch (start us, length us, event | category | flops | bytes accessed | tf_op | source)
XLA Modules:
  0.0 109.9 jit_solution(16503115233631029869)
XLA Ops:
  6.5 0.0 all-gather.2.cloned.1.call-start
  6.5 4.3 %collective-permute-start = (bf16[128,1024]{1,0:T(8,128)(2,1)}, bf16[128,1024]{1,0:T(8,128)(2,1)S(1)}, u32[]{:S(2)}, u32[]{:S(2)}) collective-permute-start(bf16[128,1024]{1,0:T(8,128)(2,1)} %param.5), channel_id=1, source_target_pairs={{0,64},{64,128},{128,192},{192,256},{256,320},{320,384},{384,448},... | collective-permute-start | bytes 786440 | tf_op jit(solution)/shard_map/ppermute | solution.py:25
  10.8 10.0 %collective-permute-start.1 = (bf16[128,1024]{1,0:T(8,128)(2,1)}, bf16[128,1024]{1,0:T(8,128)(2,1)S(1)}, u32[]{:S(2)}, u32[]{:S(2)}) collective-permute-start(bf16[128,1024]{1,0:T(8,128)(2,1)} %param.5), channel_id=1, source_target_pairs={{0,384},{64,448},{128,0},{192,64},{256,128},{320,192},{384,256},{4... | collective-permute-start | bytes 786440 | tf_op jit(solution)/shard_map/ppermute | solution.py:25
  20.9 0.7 fusion.2.place
  21.6 1.9 %pad_maximum_fusion = bf16[256,1024]{1,0:T(8,128)(2,1)} fusion(bf16[128,1024]{1,0:T(8,128)(2,1)} %param.6, bf16[128,1024]{1,0:T(8,128)(2,1)} %param.5), kind=kLoop, calls=%fused_computation.1 | loop fusion | flops 1048576 | bytes 1048576 | tf_op jit(solution)/shard_map/concatenate | solution.py:168
  23.4 0.6 collective-permute-done
  24.0 1.9 %collective-permute-start.2 = (bf16[128,1024]{1,0:T(8,128)(2,1)S(1)}, bf16[128,1024]{1,0:T(8,128)(2,1)S(1)}, u32[]{:S(2)}, u32[]{:S(2)}) collective-permute-start(bf16[128,1024]{1,0:T(8,128)(2,1)S(1)} %collective-permute-done), channel_id=1, source_target_pairs={{0,64},{64,128},{128,192},{192,256},{256,320},{320,384},{384,448},... | collective-permute-start | bytes 786440 | tf_op jit(solution)/shard_map/ppermute | solution.py:25
  25.9 1.0 constant_dynamic-update-slice_fusion.2
  27.6 4.3 %collective-permute-done.1 = bf16[128,1024]{1,0:T(8,128)(2,1)S(1)} collective-permute-done((bf16[128,1024]{1,0:T(8,128)(2,1)}, bf16[128,1024]{1,0:T(8,128)(2,1)S(1)}, u32[]{:S(2)}, u32[]{:S(2)}) %collective-permute-start.1) | collective-permute-done | bytes 262176 | tf_op jit(solution)/shard_map/ppermute | solution.py:25
  31.9 2.7 %collective-permute-done.2.a2 = bf16[128,1024]{1,0:T(8,128)(2,1)S(1)} collective-permute-done((bf16[128,1024]{1,0:T(8,128)(2,1)S(1)}, bf16[128,1024]{1,0:T(8,128)(2,1)S(1)}, u32[]{:S(2)}, u32[]{:S(2)}) %collective-permute-start.2) | collective-permute-done | bytes 262176 | tf_op jit(solution)/shard_map/ppermute | solution.py:25
  34.6 0.0 all-gather.2.cloned.1.call-update
  34.6 1.9 %collective-permute-start.3 = (bf16[384,1024]{1,0:T(8,128)(2,1)S(1)}, bf16[384,1024]{1,0:T(8,128)(2,1)S(1)}, u32[]{:S(2)}, u32[]{:S(2)}) collective-permute-start(bf16[384,1024]{1,0:T(8,128)(2,1)S(1)} %constant_dynamic-update-slice_fusion.a.near), channel_id=1, source_target_pairs={{0,32},{32,0},{1,33},{33,1},{2,34},{34,2},{3,35},{35,3},{4,36},{36... | collective-permute-start | bytes 2359304 | tf_op jit(solution)/shard_map/ppermute | solution.py:29
  36.5 2.3 %collective-permute-done.3.b.near_b = bf16[384,1024]{1,0:T(8,128)(2,1)S(1)} collective-permute-done((bf16[384,1024]{1,0:T(8,128)(2,1)S(1)}, bf16[384,1024]{1,0:T(8,128)(2,1)S(1)}, u32[]{:S(2)}, u32[]{:S(2)}) %collective-permute-start.3) | collective-permute-done | bytes 786464 | tf_op jit(solution)/shard_map/ppermute | solution.py:29
  38.8 2.1 %shard_map.55 = bf16[32,64,128]{2,1,0:T(8,128)(2,1)S(1)} custom-call(bf16[384,1024]{1,0:T(8,128)(2,1)S(1)} %constant_dynamic-update-slice_fusion.a.near, bf16[384,1024]{1,0:T(8,128)(2,1)S(1)} %collective-permute-done.3.b.near_b, bf16[128,1024]{1,0:T(8,128)(2,1)S(1)} %collective-permute-done.2.a2), custom_call_target="tpu_custom_call" | custom-call | flops 805306368 | bytes 2621440 | tf_op jit(solution)/shard_map/pallas_call | solution.py:68
  40.9 27.5 %all_to_all.10 = bf16[32,64,128]{2,1,0:T(8,128)(2,1)S(1)} all-to-all(bf16[32,64,128]{2,1,0:T(8,128)(2,1)S(1)} %shard_map.55), channel_id=1, replica_groups=mesh['z'=8,'core'=2,'y'=8,'x'=4] {'y','x'}, dimensions={0} | all-to-all | bytes 1048576 | tf_op jit(solution)/shard_map/all_to_all | solution.py:178
  68.4 0.1 convert_reduce_fusion
  68.5 0.7 collective-permute-start.4
  69.2 0.0 collective-permute-done.4
  69.2 0.1 broadcast_in_dim.2
  69.3 28.6 %all_to_all.11.slots = bf16[32,64,128]{2,1,0:T(8,128)(2,1)S(1)} all-to-all(bf16[32,64,128]{2,1,0:T(8,128)(2,1)S(1)} %broadcast_in_dim.2), channel_id=1, replica_groups=mesh['z'=8,'core'=2,'y'=8,'x'=4] {'y','x'}, dimensions={0} | all-to-all | bytes 1048576 | tf_op jit(solution)/shard_map/all_to_all | solution.py:182
  97.9 0.0 all-gather.2.cloned.1.call-done
  97.9 5.2 %shard_map.56 = f32[128,1024]{1,0:T(8,128)} custom-call(s32[16]{0:T(128)S(1)} %fusion.2.place, f32[1]{0:T(128)S(6)} %mul.12.half, bf16[32,64,128]{2,1,0:T(8,128)(2,1)S(1)} %all_to_all.11.slots, bf16[384,1024]{1,0:T(8,128)(2,1)S(1)} %constant_dynamic-update-slice_fusion.a.near, bf16[384,1024]{1,0:T(8,128)(2,1)S(1)} %collective-permute-done.3.b.near_b, ...), custom_call_target="tpu_custom_call" | custom-call | flops 1073741824 | bytes 10485760 | tf_op jit(solution)/shard_map/pallas_call | solution.py:126
  (3 shorter events, 0.1 us)
Async XLA Ops:
  6.5 91.3 %all-gather.2.cloned.1.call-start = ((), (), s32[]{:S(2)}) async-start(), calls=%async_computation.2 | async-start | bytes 8912896 | tf_op jit(solution)/shard_map/all_gather | solution.py:176
  6.5 17.4 %collective-permute-start = (bf16[128,1024]{1,0:T(8,128)(2,1)}, bf16[128,1024]{1,0:T(8,128)(2,1)S(1)}, u32[]{:S(2)}, u32[]{:S(2)}) collective-permute-start(bf16[128,1024]{1,0:T(8,128)(2,1)} %param.5), channel_id=1, source_target_pairs={{0,64},{64,128},{128,192},{192,256},{256,320},{320,384},{384,448},... | collective-permute-start | bytes 786440 | tf_op jit(solution)/shard_map/ppermute | solution.py:25
  10.8 21.0 %collective-permute-start.1 = (bf16[128,1024]{1,0:T(8,128)(2,1)}, bf16[128,1024]{1,0:T(8,128)(2,1)S(1)}, u32[]{:S(2)}, u32[]{:S(2)}) collective-permute-start(bf16[128,1024]{1,0:T(8,128)(2,1)} %param.5), channel_id=1, source_target_pairs={{0,384},{64,448},{128,0},{192,64},{256,128},{320,192},{384,256},{4... | collective-permute-start | bytes 786440 | tf_op jit(solution)/shard_map/ppermute | solution.py:25
  24.0 10.6 %collective-permute-start.2 = (bf16[128,1024]{1,0:T(8,128)(2,1)S(1)}, bf16[128,1024]{1,0:T(8,128)(2,1)S(1)}, u32[]{:S(2)}, u32[]{:S(2)}) collective-permute-start(bf16[128,1024]{1,0:T(8,128)(2,1)S(1)} %collective-permute-done), channel_id=1, source_target_pairs={{0,64},{64,128},{128,192},{192,256},{256,320},{320,384},{384,448},... | collective-permute-start | bytes 786440 | tf_op jit(solution)/shard_map/ppermute | solution.py:25
  34.6 4.2 %collective-permute-start.3 = (bf16[384,1024]{1,0:T(8,128)(2,1)S(1)}, bf16[384,1024]{1,0:T(8,128)(2,1)S(1)}, u32[]{:S(2)}, u32[]{:S(2)}) collective-permute-start(bf16[384,1024]{1,0:T(8,128)(2,1)S(1)} %constant_dynamic-update-slice_fusion.a.near), channel_id=1, source_target_pairs={{0,32},{32,0},{1,33},{33,1},{2,34},{34,2},{3,35},{35,3},{4,36},{36... | collective-permute-start | bytes 2359304 | tf_op jit(solution)/shard_map/ppermute | solution.py:29
  68.5 0.7 collective-permute-start.4
Sparse Core Ops, SparseCore 0:
  34.7 57.4 all-gather.1

commit v8 on v6

--- a/solution.py
+++ b/solution.py
@@ -102,19 +102,22 @@
     kernel = jnp.concatenate(blocks, axis=1)
     weight = jnp.sum(kernel.astype(jnp.float32), axis=1, keepdims=True)
     tiles = [slice(start, start + 256) for start in range(0, COLS, 256)]
+    away = [i for i in range(NZ * NC) if i not in here]
+    for_here = jnp.concatenate([blocks[i] for i in here], axis=1)
+    for_away = jnp.concatenate([blocks[i] for i in away], axis=1)
+    for at in tiles:
+        held = [ref[j * ROWS : (j + 1) * ROWS, at] for ref, j in here.values()]
+        spread = jnp.dot(
+            for_here, jnp.concatenate(held, axis=0), preferred_element_type=jnp.float32
+        )
+        out[:, at] = weight * near[:ROWS, at].astype(jnp.float32) - spread
     for copy in copies[0]:
         copy.wait()
-
-    def coords(at):
-        parts = []
-        for i in range(NZ * NC):
-            ref, j = here.get(i, (xs, i))
-            parts.append(ref[j * ROWS : (j + 1) * ROWS, at])
-        return jnp.concatenate(parts, axis=0)
-
     for at in tiles:
-        spread = jnp.dot(kernel, coords(at), preferred_element_type=jnp.float32)
-        out[:, at] = weight * near[:ROWS, at].astype(jnp.float32) - spread
+        held = [xs[i * ROWS : (i + 1) * ROWS, at] for i in away]
+        out[:, at] -= jnp.dot(
+            for_away, jnp.concatenate(held, axis=0), preferred_element_type=jnp.float32
+        )
     for copy in copies[1]:
         copy.wait()
     for at in tiles:

time: 110 us -> 110 us (level)
  no operation moved by 1% of the time
where the time goes in v8:
time: 110 us
  blocking collectives  56 us (51%)
  starting transfers between devices  18.8 us (17%)
  between operations  14.1 us (13%)
  waiting for transfers between devices  9.85 us (9%)
  Pallas kernels  7.45 us (7%)
  other arithmetic  3.65 us (3%)
    all_to_all x1, blocking collectives, on_device(): lax.all_to_all(jnp.broadcast_to(piece[None], (NF, 64, 128)), FIELD, 0, 0,...  28.6 us
    all_to_all x1, blocking collectives, on_device(): terms = lax.all_to_all(slots, FIELD, 0, 0, tiled=True)  27.5 us
    ppermute x3, starting transfers between devices, shift(): return lax.ppermute(array, 'z', [(i, (i + hops) % NZ) for i in range(NZ)])  16.2 us
    ppermute x3, waiting for transfers between devices, shift(): return lax.ppermute(array, 'z', [(i, (i + hops) % NZ) for i in range(NZ)])  7.58 us
    pallas_call x1, Pallas kernels, update(): pl.pallas_call(update_body, out_shape=jax.ShapeDtypeStruct((ROWS, COLS),...  5.3 us
    ppermute x1, waiting for transfers between devices, other_core(): return lax.ppermute(array, 'core', [(0, 1), (1, 0)])  2.25 us
  transfers between devices with their start and end apart: 6, of which 4 were waited for; matrix products, arithmetic and copies ran while one was open for 3% of the time, Pallas kernels for 2%

profile of v8, /device:TPU:8, one launch (start us, length us, event | category | flops | bytes accessed | tf_op | source)
XLA Modules:
  0.0 110.0 jit_solution(16097637958385796111)
XLA Ops:
  6.5 0.0 all-gather.2.cloned.1.call-start
  6.5 4.3 %collective-permute-start = (bf16[128,1024]{1,0:T(8,128)(2,1)}, bf16[128,1024]{1,0:T(8,128)(2,1)S(1)}, u32[]{:S(2)}, u32[]{:S(2)}) collective-permute-start(bf16[128,1024]{1,0:T(8,128)(2,1)} %param.5), channel_id=1, source_target_pairs={{0,64},{64,128},{128,192},{192,256},{256,320},{320,384},{384,448},... | collective-permute-start | bytes 786440 | tf_op jit(solution)/shard_map/ppermute | solution.py:25
  10.8 10.0 %collective-permute-start.1 = (bf16[128,1024]{1,0:T(8,128)(2,1)}, bf16[128,1024]{1,0:T(8,128)(2,1)S(1)}, u32[]{:S(2)}, u32[]{:S(2)}) collective-permute-start(bf16[128,1024]{1,0:T(8,128)(2,1)} %param.5), channel_id=1, source_target_pairs={{0,384},{64,448},{128,0},{192,64},{256,128},{320,192},{384,256},{4... | collective-permute-start | bytes 786440 | tf_op jit(solution)/shard_map/ppermute | solution.py:25
  20.9 3.1 %collective-permute-done = bf16[128,1024]{1,0:T(8,128)(2,1)S(1)} collective-permute-done((bf16[128,1024]{1,0:T(8,128)(2,1)}, bf16[128,1024]{1,0:T(8,128)(2,1)S(1)}, u32[]{:S(2)}, u32[]{:S(2)}) %collective-permute-start) | collective-permute-done | bytes 262176 | tf_op jit(solution)/shard_map/ppermute | solution.py:25
  24.0 1.9 %collective-permute-start.2 = (bf16[128,1024]{1,0:T(8,128)(2,1)S(1)}, bf16[128,1024]{1,0:T(8,128)(2,1)S(1)}, u32[]{:S(2)}, u32[]{:S(2)}) collective-permute-start(bf16[128,1024]{1,0:T(8,128)(2,1)S(1)} %collective-permute-done), channel_id=1, source_target_pairs={{0,64},{64,128},{128,192},{192,256},{256,320},{320,384},{384,448},... | collective-permute-start | bytes 786440 | tf_op jit(solution)/shard_map/ppermute | solution.py:25
  25.9 0.7 fusion.2.place
  27.2 1.9 %pad_maximum_fusion.1 = bf16[256,1024]{1,0:T(8,128)(2,1)} fusion(bf16[128,1024]{1,0:T(8,128)(2,1)} %param.6, bf16[128,1024]{1,0:T(8,128)(2,1)} %param.5), kind=kLoop, calls=%fused_computation.2 | loop fusion | flops 1048576 | bytes 1048576 | tf_op jit(solution)/shard_map/concatenate | solution.py:171
  29.1 2.7 %collective-permute-done.1 = bf16[128,1024]{1,0:T(8,128)(2,1)S(1)} collective-permute-done((bf16[128,1024]{1,0:T(8,128)(2,1)}, bf16[128,1024]{1,0:T(8,128)(2,1)S(1)}, u32[]{:S(2)}, u32[]{:S(2)}) %collective-permute-start.1) | collective-permute-done | bytes 262176 | tf_op jit(solution)/shard_map/ppermute | solution.py:25
  31.8 1.0 pad_maximum_fusion.a.near
  32.8 1.7 %collective-permute-done.2.a2 = bf16[128,1024]{1,0:T(8,128)(2,1)S(1)} collective-permute-done((bf16[128,1024]{1,0:T(8,128)(2,1)S(1)}, bf16[128,1024]{1,0:T(8,128)(2,1)S(1)}, u32[]{:S(2)}, u32[]{:S(2)}) %collective-permute-start.2) | collective-permute-done | bytes 262176 | tf_op jit(solution)/shard_map/ppermute | solution.py:25
  34.6 0.0 all-gather.2.cloned.1.call-update
  34.6 1.9 %collective-permute-start.3 = (bf16[384,1024]{1,0:T(8,128)(2,1)S(1)}, bf16[384,1024]{1,0:T(8,128)(2,1)S(1)}, u32[]{:S(2)}, u32[]{:S(2)}) collective-permute-start(bf16[384,1024]{1,0:T(8,128)(2,1)S(1)} %pad_maximum_fusion.a.near), channel_id=1, source_target_pairs={{0,32},{32,0},{1,33},{33,1},{2,34},{34,2},{3,35},{35,3},{4,36},{36... | collective-permute-start | bytes 2359304 | tf_op jit(solution)/shard_map/ppermute | solution.py:29
  36.5 2.3 %collective-permute-done.3.b.near_b = bf16[384,1024]{1,0:T(8,128)(2,1)S(1)} collective-permute-done((bf16[384,1024]{1,0:T(8,128)(2,1)S(1)}, bf16[384,1024]{1,0:T(8,128)(2,1)S(1)}, u32[]{:S(2)}, u32[]{:S(2)}) %collective-permute-start.3) | collective-permute-done | bytes 786464 | tf_op jit(solution)/shard_map/ppermute | solution.py:29
  38.8 2.1 %shard_map.55 = bf16[32,64,128]{2,1,0:T(8,128)(2,1)S(1)} custom-call(bf16[384,1024]{1,0:T(8,128)(2,1)S(1)} %pad_maximum_fusion.a.near, bf16[384,1024]{1,0:T(8,128)(2,1)S(1)} %collective-permute-done.3.b.near_b, bf16[128,1024]{1,0:T(8,128)(2,1)S(1)} %collective-permute-done.2.a2), custom_call_target="tpu_custom_call" | custom-call | flops 805306368 | bytes 2621440 | tf_op jit(solution)/shard_map/pallas_call | solution.py:68
  40.9 27.5 %all_to_all.10 = bf16[32,64,128]{2,1,0:T(8,128)(2,1)S(1)} all-to-all(bf16[32,64,128]{2,1,0:T(8,128)(2,1)S(1)} %shard_map.55), channel_id=1, replica_groups=mesh['z'=8,'core'=2,'y'=8,'x'=4] {'y','x'}, dimensions={0} | all-to-all | bytes 1048576 | tf_op jit(solution)/shard_map/all_to_all | solution.py:181
  68.4 0.1 convert_reduce_fusion
  68.5 0.7 collective-permute-start.4
  69.2 0.0 collective-permute-done.4
  69.2 0.1 broadcast_in_dim.2
  69.3 28.6 %all_to_all.11.slots = bf16[32,64,128]{2,1,0:T(8,128)(2,1)S(1)} all-to-all(bf16[32,64,128]{2,1,0:T(8,128)(2,1)S(1)} %broadcast_in_dim.2), channel_id=1, replica_groups=mesh['z'=8,'core'=2,'y'=8,'x'=4] {'y','x'}, dimensions={0} | all-to-all | bytes 1048576 | tf_op jit(solution)/shard_map/all_to_all | solution.py:185
  97.9 0.0 all-gather.2.cloned.1.call-done
  97.9 5.3 %shard_map.56 = f32[128,1024]{1,0:T(8,128)} custom-call(s32[16]{0:T(128)S(1)} %fusion.2.place, f32[1]{0:T(128)S(6)} %mul.12.half, bf16[32,64,128]{2,1,0:T(8,128)(2,1)S(1)} %all_to_all.11.slots, bf16[384,1024]{1,0:T(8,128)(2,1)S(1)} %pad_maximum_fusion.a.near, bf16[384,1024]{1,0:T(8,128)(2,1)S(1)} %collective-permute-done.3.b.near_b, ...), custom_call_target="tpu_custom_call" | custom-call | flops 1073741824 | bytes 10485760 | tf_op jit(solution)/shard_map/pallas_call | solution.py:129
  (1 shorter events, 0.0 us)
Async XLA Ops:
  6.5 91.3 %all-gather.2.cloned.1.call-start = ((), (), s32[]{:S(2)}) async-start(), calls=%async_computation.2 | async-start | bytes 8912896 | tf_op jit(solution)/shard_map/all_gather | solution.py:178
  6.5 17.4 %collective-permute-start = (bf16[128,1024]{1,0:T(8,128)(2,1)}, bf16[128,1024]{1,0:T(8,128)(2,1)S(1)}, u32[]{:S(2)}, u32[]{:S(2)}) collective-permute-start(bf16[128,1024]{1,0:T(8,128)(2,1)} %param.5), channel_id=1, source_target_pairs={{0,64},{64,128},{128,192},{192,256},{256,320},{320,384},{384,448},... | collective-permute-start | bytes 786440 | tf_op jit(solution)/shard_map/ppermute | solution.py:25
  10.8 21.0 %collective-permute-start.1 = (bf16[128,1024]{1,0:T(8,128)(2,1)}, bf16[128,1024]{1,0:T(8,128)(2,1)S(1)}, u32[]{:S(2)}, u32[]{:S(2)}) collective-permute-start(bf16[128,1024]{1,0:T(8,128)(2,1)} %param.5), channel_id=1, source_target_pairs={{0,384},{64,448},{128,0},{192,64},{256,128},{320,192},{384,256},{4... | collective-permute-start | bytes 786440 | tf_op jit(solution)/shard_map/ppermute | solution.py:25
  24.0 10.6 %collective-permute-start.2 = (bf16[128,1024]{1,0:T(8,128)(2,1)S(1)}, bf16[128,1024]{1,0:T(8,128)(2,1)S(1)}, u32[]{:S(2)}, u32[]{:S(2)}) collective-permute-start(bf16[128,1024]{1,0:T(8,128)(2,1)S(1)} %collective-permute-done), channel_id=1, source_target_pairs={{0,64},{64,128},{128,192},{192,256},{256,320},{320,384},{384,448},... | collective-permute-start | bytes 786440 | tf_op jit(solution)/shard_map/ppermute | solution.py:25
  34.6 4.2 %collective-permute-start.3 = (bf16[384,1024]{1,0:T(8,128)(2,1)S(1)}, bf16[384,1024]{1,0:T(8,128)(2,1)S(1)}, u32[]{:S(2)}, u32[]{:S(2)}) collective-permute-start(bf16[384,1024]{1,0:T(8,128)(2,1)S(1)} %pad_maximum_fusion.a.near), channel_id=1, source_target_pairs={{0,32},{32,0},{1,33},{33,1},{2,34},{34,2},{3,35},{35,3},{4,36},{36... | collective-permute-start | bytes 2359304 | tf_op jit(solution)/shard_map/ppermute | solution.py:29
  68.5 0.7 collective-permute-start.4
Sparse Core Ops, SparseCore 0:
  34.7 57.6 all-gather.1
